TPU v7x, 32 devices: a whole 2x2x4 slice. The times are simulated.
32 devices in a mesh: dp: 4 (over y, x), fsdp: 8 (over z, core).
Axes of the slice: x: 2, y: 2, z: 4, core: 2. Of those that a mesh axis runs over, the one named last changes fastest.
Arguments:
- inputs: bfloat16 [65536, 1280], P(('dp', 'fsdp')), may hold values from -6 to 6
- lengths: int32 [32, 8], P(('dp', 'fsdp')), may hold values from 1 to 1024, 2048 in all within a row
- keep_mask: int32 [65536], P(('dp', 'fsdp')), may hold values 0 or 1
- cotangent: bfloat16 [65536, 1280], P(('dp', 'fsdp')), may hold values from -6 to 6
- ln1_gain: bfloat16 [1280], P(('dp', 'fsdp')), may hold values from 0.099609375 to 1.8984375
- ln1_bias: bfloat16 [1280], P(('dp', 'fsdp')), may hold values from -3 to 3
- up_weight: bfloat16 [1280, 640], P(('dp', 'fsdp')), may hold values from -0.15625 to 0.15625
- up_bias: bfloat16 [640], P(('dp', 'fsdp')), may hold values from -3 to 3
- ln2_gain: bfloat16 [640], P(('dp', 'fsdp')), may hold values from 0.099609375 to 1.8984375
- ln2_bias: bfloat16 [640], P(('dp', 'fsdp')), may hold values from -3 to 3
- conv_weight: bfloat16 [5, 640, 640], P(None, ('dp', 'fsdp')), may hold values from -0.109375 to 0.109375
- conv_bias: bfloat16 [640], P(('dp', 'fsdp')), may hold values from -3 to 3
- ln3_gain: bfloat16 [640], P(('dp', 'fsdp')), may hold values from 0.099609375 to 1.8984375
- ln3_bias: bfloat16 [640], P(('dp', 'fsdp')), may hold values from -3 to 3
- down_weight: bfloat16 [640, 1280], P(None, ('dp', 'fsdp')), may hold values from -0.3125 to 0.3125
- down_bias: bfloat16 [1280], P(('dp', 'fsdp')), may hold values from -3 to 3
Outputs:
- output: bfloat16 [65536, 1280], P(('dp', 'fsdp'))
- input_grad: float32 [65536, 1280], P(('dp', 'fsdp'))
- up_weight_grad: float32 [1280, 640], P(('dp', 'fsdp'))
- conv_weight_grad: float32 [5, 640, 640], P(None, ('dp', 'fsdp'))
- down_weight_grad: float32 [640, 1280], P(None, ('dp', 'fsdp'))
- ln1_gain_grad: float32 [1280], P(('dp', 'fsdp'))
- ln1_bias_grad: float32 [1280], P(('dp', 'fsdp'))
- up_bias_grad: float32 [640], P(('dp', 'fsdp'))
- ln2_gain_grad: float32 [640], P(('dp', 'fsdp'))
- ln2_bias_grad: float32 [640], P(('dp', 'fsdp'))
- conv_bias_grad: float32 [640], P(('dp', 'fsdp'))
- ln3_gain_grad: float32 [640], P(('dp', 'fsdp'))
- ln3_bias_grad: float32 [640], P(('dp', 'fsdp'))
- down_bias_grad: float32 [1280], P(('dp', 'fsdp'))
Inputs may be any that keep to these rules, and one draw needn't show every extreme that they name: `lengths`: each row sums to 2048; the largest entry of every row is 1024.
All inputs are finite; a program needn't handle non-finite values. No bound on the sum of `keep_mask` on one device may be relied on, other than what follows from the above.
Results may differ from a plain program's by a relative error of at most 0.0068.
Values may be sent and summed in bfloat16 or wider, within the bound.
No kernel may reach another device: no remote copies, remote signals or barrier semaphores. Data moves between devices by JAX's collectives and lax.ppermute only.
A program may use at most 192 MiB of HBM per device.

v0:
```python
import functools

import jax
import jax.numpy as jnp
from jax import lax
from jax.experimental import pallas as pl
from jax.experimental.pallas import tpu as pltpu
from jax.sharding import Mesh
from jax.sharding import PartitionSpec as P

KERNEL = 5
DILATION = 8
REACH = KERNEL // 2 * DILATION
ALL = ("dp", "chip", "core")
F32 = jnp.float32
BF16 = jnp.bfloat16
TANH_ONE = 0.7978845608028654
TANH_THREE = TANH_ONE * 0.044715
ROWS = 32
VMEM_MIB = {"first_act": 24, "up": 14, "conv": 40, "weights": 44, "mid_grad": 24, "up_weight": 30, "input_grad": 20, "output": 12}


def swap(array, axis, size, mask):
    return lax.ppermute(array, axis, [(k, k ^ mask) for k in range(size)])


def after(value, *others):
    return lax.optimization_barrier((value, *others))[0]


def gather_stage(block, axis):
    name, size = axis
    return [block] + [swap(block, name, size, mask) for mask in range(1, size)]


def core_stage(pieces, axes):
    return pieces + [swap(piece, axes[2][0], axes[2][1], 1) for piece in pieces]


def scatter_stage(total, axis):
    name, size = axis
    arrived = [swap(total[mask].astype(BF16), name, size, mask) for mask in range(1, size)]
    return total[0], arrived


def add_up(kept, arrived):
    total = kept.astype(F32)
    for item in arrived:
        total = total + item.astype(F32)
    return total


def exact_stage(total, axis):
    name, size = axis
    return total[0] + sum(swap(total[mask], name, size, mask) for mask in range(1, size))


def norm(z, width):
    center = z - jnp.sum(z, axis=1, keepdims=True) * (1.0 / width)
    scale = lax.rsqrt(jnp.sum(center * center, axis=1, keepdims=True) * (1.0 / width) + 1e-05)
    return center * scale, scale


def pipelined(product, rest, keep):
    step, last = pl.program_id(0), pl.num_programs(0) - 1

    @pl.when(step == 0)
    def _():
        product()
        keep()

    @pl.when((step > 0) & (step < last))
    def _():
        product()
        rest()
        keep()

    @pl.when(step == last)
    def _():
        rest()


def half_gelu(h):
    q = h * h
    t = jnp.tanh(h * (2.0 * TANH_ONE + 8.0 * TANH_THREE * q))
    return q, t, 1.0 + t


def double_slope(h, q, t, one_t):
    return one_t * (1.0 + (1.0 - t) * (h * (2.0 * TANH_ONE + 24.0 * TANH_THREE * q)))


def back_parts(hat, scale, half_gain, slope2, grad, width):
    by_sum = slope2 * grad
    by_gain = by_sum * hat
    by_hat = by_sum * half_gain
    first = jnp.sum(by_hat, axis=1, keepdims=True) * (scale * (1.0 / width))
    second = jnp.sum(by_hat * hat, axis=1, keepdims=True) * (scale * (1.0 / width))
    return scale * by_hat - first - hat * second, by_gain, by_sum


def fold(value):
    return sum(value[k : k + 8] for k in range(0, value.shape[0], 8))


def chunks(count, body, unroll=4):
    def step(k, carry):
        body(pl.multiple_of(k * ROWS, ROWS))
        return carry

    lax.fori_loop(0, count // ROWS, step, 0, unroll=unroll)


def dot(left, right, left_dim=1, right_dim=0):
    return lax.dot_general(
        left, right, (((left_dim,), (right_dim,)), ((), ())), preferred_element_type=F32
    )


def piece_copies(pieces, place_ref, hold_ref, semaphores):
    half = len(pieces) // 2
    columns = pieces[0].shape[0]
    copies = []
    for c in range(2):
        for o in range(half):
            for i in range(columns):
                chip = (place_ref[0] ^ o) * columns + (place_ref[1] ^ i)
                target = hold_ref.at[2 * chip + (place_ref[2] ^ c)]
                copies.append(pltpu.make_async_copy(pieces[c * half + o].at[i], target, semaphores.at[len(copies)]))
    return copies


def first_act_kernel(
    own_pieces, other_pieces, x_ref, place_ref,
    act_ref, up_ref, down_ref, wide_ref, narrow_ref, hold_ref, up_wide_ref, down_wide_ref, semaphores,
):
    block, width = x_ref.shape

    @pl.when(pl.program_id(0) == 0)
    def _():
        parts = [piece.at[o] for piece in (own_pieces, other_pieces) for o in range(piece.shape[0])]
        copies = piece_copies(parts, place_ref, hold_ref, semaphores)
        for copy in copies:
            copy.start()
        for copy in copies:
            copy.wait()
        devices = hold_ref.shape[0]
        share, of_narrow = width // devices, narrow_ref.shape[1] // devices
        for k in range(devices):
            item = hold_ref[k].astype(F32)
            small = item[item.shape[0] - 8 :, :]
            wide_ref[:, k * share : (k + 1) * share] = small[:, 0:share]
            narrow_ref[:, k * of_narrow : (k + 1) * of_narrow] = small[:, 128 : 128 + of_narrow]
            up_wide_ref[k * share : (k + 1) * share, :] = item[0:share, :]
            down_wide_ref[k * share : (k + 1) * share, :] = item[share : 2 * share, :]
        up_ref[...] = up_wide_ref[...].astype(BF16)
        down_ref[...] = down_wide_ref[...].astype(BF16)

    gain, bias = 0.5 * wide_ref[0:1, :], 0.5 * wide_ref[1:2, :]

    def body(at):
        hat, _ = norm(x_ref[pl.ds(at, ROWS), :].astype(F32), width)
        h = hat * gain + bias
        act_ref[pl.ds(at, ROWS), :] = (h * half_gelu(h)[2]).astype(BF16)

    chunks(block, body)


def up_kernel(act_ref, weight_ref, narrow_ref, flags_ref, out_ref, mid_ref, z_ref, next_ref):
    block, width = out_ref.shape

    def product():
        next_ref[...] = dot(act_ref[...], weight_ref[...])

    def keep():
        z_ref[...] = next_ref[...]

    def rest():
        shift, gain, bias = narrow_ref[0:1, :], 0.5 * narrow_ref[1:2, :], 0.5 * narrow_ref[2:3, :]
        for at in range(0, block, ROWS):
            rows = slice(at, at + ROWS)
            z = z_ref[rows, :] + shift
            out_ref[rows, :] = z
            hat, _ = norm(z, width)
            h = hat * gain + bias
            mid_ref[rows, :] = (h * half_gelu(h)[2] * flags_ref[rows, 0:1]).astype(BF16)

    pipelined(product, rest, keep)


def fill_padded(padded_ref, source_ref):
    count, width = source_ref.shape
    padded_ref[0, 0:REACH, :] = jnp.zeros((REACH, width), BF16)
    padded_ref[0, count + REACH : count + 2 * REACH, :] = jnp.zeros((REACH, width), BF16)
    padded_ref[0, REACH : count + REACH, :] = source_ref[...]
    padded_ref[1, 0 : count + REACH, :] = padded_ref[0, DILATION : count + REACH + DILATION, :]


def shifted(padded_ref, flags, start, block, tap):
    which, at = tap % 2, start + tap // 2 * (2 * DILATION)
    if not isinstance(at, int):
        at = pl.multiple_of(at, 2 * DILATION)
    rows = padded_ref[which, pl.ds(at, block), :]
    if tap != KERNEL // 2:
        rows = rows * flags[:, tap + 1 : tap + 2]
    return rows


def conv_kernel(*refs):
    pieces, rest_refs = refs[: len(refs) - 22], refs[len(refs) - 22 :]
    (
        mid_ref, down_ref, cot_ref, narrow_ref, now_flags_ref, place_ref,
        top_ref, low_ref, flat_hbm, sums_ref, wide_sums_ref,
        padded_ref, hold_ref, wide_weight_ref, weight_ref, flat_ref, taps_ref,
        out_ref, grad_ref, next_out_ref, next_grad_ref, semaphores,
    ) = rest_refs
    step = pl.program_id(0)
    block, width = out_ref.shape
    devices = hold_ref.shape[0]
    share = width // devices
    flat_copy = pltpu.make_async_copy(flat_ref, flat_hbm, semaphores.at[devices])

    @pl.when(step == 0)
    def _():
        copies = piece_copies(pieces, place_ref, hold_ref, semaphores)
        for copy in copies:
            copy.start()
        fill_padded(padded_ref, mid_ref)
        sums_ref[...] = jnp.zeros_like(sums_ref)
        wide_sums_ref[...] = jnp.zeros_like(wide_sums_ref)
        for copy in copies:
            copy.wait()
        for tap in range(KERNEL):
            for k in range(devices):
                item = hold_ref[k].astype(F32)
                wide_weight_ref[tap % 2, k * share : (k + 1) * share, :] = item[tap * share : (tap + 1) * share, :]
            part = wide_weight_ref[tap % 2].astype(BF16)
            weight_ref[tap * width : (tap + 1) * width, :] = part
            flat_ref[:, tap * width : (tap + 1) * width] = part
        flat_copy.start()

    def product():
        start = jnp.minimum(step, pl.num_programs(0) - 2) * block
        flags = now_flags_ref[...].astype(BF16)
        for tap in range(KERNEL):
            taps_ref[:, tap * width : (tap + 1) * width] = shifted(padded_ref, flags, start, block, tap)
        next_out_ref[...] = dot(taps_ref[...], weight_ref[...])
        next_grad_ref[...] = dot(cot_ref[...], down_ref[...])
        total = wide_sums_ref[...]
        for at in range(0, block, ROWS):
            total += fold(cot_ref[at : at + ROWS, :].astype(F32))
        wide_sums_ref[...] = total

    def keep():
        out_ref[...] = next_out_ref[...]
        grad_ref[...] = next_grad_ref[...]

    def rest():
        shift, gain, bias = narrow_ref[3:4, :], 0.5 * narrow_ref[4:5, :], 0.5 * narrow_ref[5:6, :]
        totals = [sums_ref[8 * k : 8 * k + 8, :] for k in range(3)]
        for at in range(0, block, ROWS):
            rows = slice(at, at + ROWS)
            hat, scale = norm(out_ref[rows, :] + shift, width)
            h = hat * gain + bias
            q, t, one_t = half_gelu(h)
            top_ref[rows, :] = (h * one_t).astype(BF16)
            slope2 = double_slope(h, q, t, one_t)
            back, by_gain, by_sum = back_parts(hat, scale, gain, slope2, grad_ref[rows, :], width)
            low_ref[rows, :] = back.astype(BF16)
            for k, part in enumerate((by_gain, by_sum, back)):
                totals[k] += fold(part)
        for k in range(3):
            sums_ref[8 * k : 8 * k + 8, :] = totals[k]

    pipelined(product, rest, keep)

    @pl.when(step == pl.num_programs(0) - 1)
    def _():
        flat_copy.wait()


def hand_out(place_ref, device, columns, ready_ref, rows, part):
    chip = device // 2
    m, n = (chip // columns) ^ place_ref[0], (chip % columns) ^ place_ref[1]
    which = (device % 2) ^ place_ref[2]
    if isinstance(rows, int):
        ready_ref[which, m, n, rows] = part.astype(ready_ref.dtype)
    else:
        ready_ref[which, m, n, rows, 0 : part.shape[1]] = part.astype(ready_ref.dtype)


def send_out(ready_ref, kept_hbm, sent_hbm, semaphores):
    copies = [
        pltpu.make_async_copy(ready_ref.at[k], target, semaphores.at[k])
        for k, target in enumerate((kept_hbm, sent_hbm))
    ]
    for copy in copies:
        copy.start()
    for copy in copies:
        copy.wait()


def weights_kernel(
    low_ref, mid_ref, flags_ref, place_ref, kept_hbm, sent_hbm,
    padded_ref, taps_ref, total_ref, row_ref, ready_ref, out_semaphores,
):
    count, width = mid_ref.shape
    columns = ready_ref.shape[2]
    devices = 2 * ready_ref.shape[1] * columns
    share = width // devices
    fill_padded(padded_ref, low_ref)
    flags = flags_ref[...].astype(BF16)
    for tap in range(KERNEL):
        taps_ref[:, tap * width : (tap + 1) * width] = shifted(padded_ref, flags, 0, count, KERNEL - 1 - tap)
    total_ref[...] = dot(mid_ref[...].T, taps_ref[...])
    row_ref[...] = jnp.zeros_like(row_ref)
    for device in range(devices):
        slot = device % row_ref.shape[0]
        for tap in range(KERNEL):
            part = total_ref[device * share : (device + 1) * share, tap * width : (tap + 1) * width]
            row_ref[slot, tap * share : (tap + 1) * share, :] = part
        hand_out(place_ref, device, columns, ready_ref, slice(None), row_ref[slot])
    send_out(ready_ref, kept_hbm, sent_hbm, out_semaphores)


def up_weight_kernel(
    act_ref, cot_ref, low_ref, top_ref, place_ref, kept_hbm, sent_hbm, total_ref, ready_ref, out_semaphores
):
    step, steps = pl.program_id(0), pl.num_programs(0)
    share = ready_ref.shape[4]
    devices = total_ref.shape[0] // share

    def part_of(group, left_ref, right_ref):
        total_ref[...] = dot(left_ref[...], right_ref[...], 0, 0)
        first = lax.rem(step, steps // 2) * devices
        for k in range(devices):
            part = total_ref[k * share : (k + 1) * share, :]
            hand_out(place_ref, first + k, ready_ref.shape[2], ready_ref, group, part)

    @pl.when(step < steps // 2)
    def _():
        part_of(0, act_ref, low_ref)

    @pl.when(step >= steps // 2)
    def _():
        part_of(1, cot_ref, top_ref)

    @pl.when(step == steps - 1)
    def _():
        send_out(ready_ref, kept_hbm, sent_hbm, out_semaphores)


def mid_grad_kernel(
    low_ref, flat_ref, up_out_ref, narrow_ref, now_flags_ref, flags_ref,
    up_low_ref, sums_ref,
    padded_ref, taps_ref, grad_ref, next_ref,
):
    step = pl.program_id(0)
    block, width = up_out_ref.shape

    @pl.when(step == 0)
    def _():
        fill_padded(padded_ref, low_ref)
        sums_ref[...] = jnp.zeros_like(sums_ref)

    def product():
        start = jnp.minimum(step, pl.num_programs(0) - 2) * block
        flags = now_flags_ref[...].astype(BF16)
        for tap in range(KERNEL):
            taps_ref[:, tap * width : (tap + 1) * width] = shifted(padded_ref, flags, start, block, KERNEL - 1 - tap)
        next_ref[...] = dot(taps_ref[...], flat_ref[...], 1, 1)

    def keep():
        grad_ref[...] = next_ref[...]

    def rest():
        gain, bias = 0.5 * narrow_ref[1:2, :], 0.5 * narrow_ref[2:3, :]
        totals = [sums_ref[8 * k : 8 * k + 8, :] for k in range(3)]
        for at in range(0, block, ROWS):
            rows = slice(at, at + ROWS)
            hat, scale = norm(up_out_ref[rows, :], width)
            h = hat * gain + bias
            slope2 = double_slope(h, *half_gelu(h))
            grad = grad_ref[rows, :] * flags_ref[rows, 0:1]
            back, by_gain, by_sum = back_parts(hat, scale, gain, slope2, grad, width)
            up_low_ref[rows, :] = back.astype(BF16)
            for k, part in enumerate((by_gain, by_sum, back)):
                totals[k] += fold(part)
        for k in range(3):
            sums_ref[8 * k : 8 * k + 8, :] = totals[k]

    pipelined(product, rest, keep)


def input_grad_kernel(
    up_low_ref, weight_ref, x_ref, cot_ref, wide_ref, top_sums_ref, mid_sums_ref, cot_sums_ref, place_ref,
    out_ref, kept_hbm, sent_hbm,
    grad_ref, next_ref, sums_ref, wide_row_ref, narrow_row_ref, ready_ref, out_semaphores,
):
    step, steps = pl.program_id(0), pl.num_programs(0)
    block, width = out_ref.shape

    @pl.when(step == 0)
    def _():
        sums_ref[...] = jnp.zeros_like(sums_ref)

    def product():
        next_ref[...] = dot(up_low_ref[...], weight_ref[...], 1, 1)

    def keep():
        grad_ref[...] = next_ref[...]

    def rest():
        gain, bias = 0.5 * wide_ref[0:1, :], 0.5 * wide_ref[1:2, :]
        by_gains, by_sums = sums_ref[0:8, :], sums_ref[8:16, :]
        for at in range(0, block, ROWS):
            rows = slice(at, at + ROWS)
            hat, scale = norm(x_ref[rows, :].astype(F32), width)
            h = hat * gain + bias
            slope2 = double_slope(h, *half_gelu(h))
            back, by_gain, by_sum = back_parts(hat, scale, gain, slope2, grad_ref[rows, :], width)
            out_ref[rows, :] = cot_ref[rows, :].astype(F32) + back
            by_gains += fold(by_gain)
            by_sums += fold(by_sum)
        sums_ref[0:8, :] = by_gains
        sums_ref[8:16, :] = by_sums

    pipelined(product, rest, keep)

    @pl.when(step == steps - 1)
    def _():
        def row(ref, k):
            return jnp.sum(ref[8 * k : 8 * k + 8, :], axis=0, keepdims=True)

        wide_row_ref[...] = jnp.zeros_like(wide_row_ref)
        narrow_row_ref[...] = jnp.zeros_like(narrow_row_ref)
        for at, (ref, k, factor) in enumerate(((sums_ref, 0, 0.5), (sums_ref, 1, 0.5), (cot_sums_ref, 0, 1.0))):
            wide_row_ref[at : at + 1, :] = factor * row(ref, k)
        rows = (
            (mid_sums_ref, 2, 1.0),
            (mid_sums_ref, 0, 0.5),
            (mid_sums_ref, 1, 0.5),
            (top_sums_ref, 2, 1.0),
            (top_sums_ref, 0, 0.5),
            (top_sums_ref, 1, 0.5),
        )
        for at, (ref, k, factor) in enumerate(rows):
            narrow_row_ref[at : at + 1, :] = factor * row(ref, k)
        columns = ready_ref.shape[2]
        devices = 2 * ready_ref.shape[1] * columns
        wide, narrow = width // devices, narrow_row_ref.shape[1] // devices
        ready_ref[...] = jnp.zeros_like(ready_ref)
        for device in range(devices):
            wide_part = wide_row_ref[:, device * wide : (device + 1) * wide]
            narrow_part = narrow_row_ref[:, device * narrow : (device + 1) * narrow]
            hand_out(place_ref, device, columns, ready_ref, slice(0, 8), wide_part)
            hand_out(place_ref, device, columns, ready_ref, slice(8, 16), narrow_part)
        send_out(ready_ref, kept_hbm, sent_hbm, out_semaphores)


def output_kernel(x_ref, top_ref, weight_ref, wide_ref, out_ref):
    product = dot(top_ref[...], weight_ref[...], 1, 1)
    out_ref[...] = (x_ref[...].astype(F32) + product + wide_ref[2:3, :]).astype(BF16)


def call(kernel, name, grid, ins, outs, scratch, flops, args):
    def spec(shape, rows):
        if rows in ("now", "past"):
            last = grid - 2
            place = (lambda i: jnp.minimum(i, last)) if rows == "now" else (lambda i: jnp.maximum(i - 1, 0))
            return pl.BlockSpec((shape[0] // (grid - 1),) + tuple(shape[1:]), lambda i: (place(i),) + (0,) * (len(shape) - 1))
        if rows == "any":
            return pl.BlockSpec(memory_space=pl.ANY)
        if rows == "smem":
            return pl.BlockSpec(memory_space=pltpu.SMEM)
        if rows in ("early half", "late half"):
            start = 0 if rows == "early half" else grid // 2
            return pl.BlockSpec((shape[0], shape[1] // 2), lambda i: (0, jnp.clip(i - start, 0, 1)))
        if rows is None:
            return pl.BlockSpec(shape, lambda i: (0,) * len(shape), pipeline_mode=pl.Buffered(1))
        return pl.BlockSpec((rows,) + tuple(shape[1:]), lambda i: (i,) + (0,) * (len(shape) - 1))

    results = [jax.ShapeDtypeStruct(shape, kind) for shape, kind, _ in outs]
    moved = sum(a.size * a.dtype.itemsize for a in list(args) + results) if flops > 1 else 1
    return pl.pallas_call(
        kernel,
        name=name,
        grid=(grid,),
        in_specs=[spec(a.shape, rows) for a, rows in zip(args, ins)],
        out_specs=[spec(shape, rows) for shape, _, rows in outs],
        out_shape=results,
        scratch_shapes=scratch,
        compiler_params=pltpu.CompilerParams(vmem_limit_bytes=VMEM_MIB[name] * 2**20),
        cost_estimate=pl.CostEstimate(flops=flops, bytes_accessed=moved, transcendentals=0),
    )(*args)


def flags_of(lengths_row, keep_mask):
    count = keep_mask.shape[0]
    ends = jnp.cumsum(lengths_row)
    position = jnp.arange(count, dtype=jnp.int32)[:, None]

    def segment(at):
        return jnp.sum((at >= ends[None, :]).astype(jnp.int32), axis=1, keepdims=True)

    own = segment(position)
    columns = [keep_mask[:, None] != 0]
    for tap in range(KERNEL):
        source = position + (tap - KERNEL // 2) * DILATION
        columns.append((source >= 0) & (source < count) & (segment(source) == own))
    columns += [columns[0]] * (8 - len(columns))
    return jnp.concatenate([column.astype(F32) for column in columns], axis=1)


def with_small(weight, wide, narrow):
    rows, width = weight.shape
    first = -(-rows // 8) * 8
    out = jnp.pad(weight, ((0, first + 8 - rows), (0, 0)))
    for lane, group in ((0, wide), (128, narrow)):
        for k, item in enumerate(group):
            after = width - lane - item.shape[0]
            out = out + jnp.pad(item[None, :], ((first + k, 7 - k), (lane, after)))
    return out


def padded_rows(rows):
    return -(-rows // 8) * 8


def body(
    axes,
    inputs,
    lengths,
    keep_mask,
    cotangent,
    ln1_gain,
    ln1_bias,
    up_weight,
    up_bias,
    ln2_gain,
    ln2_bias,
    conv_weight,
    conv_bias,
    ln3_gain,
    ln3_bias,
    down_weight,
    down_bias,
):
    count, model = inputs.shape
    inner = up_weight.shape[1]
    dp, columns = axes[0][1], axes[1][1]
    chips = dp * columns
    place = jnp.stack([lax.axis_index(name) for name, _ in axes]).astype(jnp.int32)
    flags = flags_of(lengths[0], keep_mask)
    share, conv_share = model // (2 * chips), KERNEL * inner // (2 * chips)

    conv_rows = padded_rows(conv_share)
    up_block = with_small(
        jnp.concatenate([up_weight, down_weight.T]),
        (ln1_gain, ln1_bias, down_bias),
        (up_bias, ln2_gain, ln2_bias, conv_bias, ln3_gain, ln3_bias),
    )
    conv_block = jnp.pad(conv_weight.reshape(-1, inner), ((0, conv_rows - conv_share), (0, 0)))
    up_one = jnp.stack(gather_stage(up_block, axes[1]))
    up_two = gather_stage(up_one, axes[0])
    name, size = axes[1]
    late_block = after(conv_block, up_one)
    conv_near = [conv_block, swap(conv_block, name, size, 1)]
    conv_near += [swap(late_block, name, size, mask) for mask in range(2, size)]
    conv_one = jnp.stack(after(tuple(conv_near), *up_two))
    conv_two = gather_stage(conv_one, axes[0])
    up_pieces = core_stage([jnp.stack(after(tuple(up_two), *conv_near))], axes)

    block = 256
    steps = count // block
    wide_up = 2 * count * model * inner
    wide_conv = 2 * count * KERNEL * inner * inner
    padded = pltpu.VMEM((2, count + 2 * REACH, inner), BF16)

    act_one, up_full, down_full, wide, narrow = call(
        first_act_kernel, "first_act", steps, ("any", "any", block, "smem"),
        [
            ((count, model), BF16, block),
            ((model, inner), BF16, None),
            ((model, inner), BF16, None),
            ((8, model), F32, None),
            ((8, inner), F32, None),
        ],
        [
            pltpu.VMEM((2 * chips,) + up_block.shape, BF16),
            pltpu.VMEM((model, inner), F32),
            pltpu.VMEM((model, inner), F32),
            pltpu.SemaphoreType.DMA((2 * chips,)),
        ],
        20 * count * model, (*up_pieces, inputs, after(place, conv_one)),
    )
    up_out, mid = call(
        up_kernel, "up", steps + 1, ("now", None, None, "past"),
        [((count, inner), F32, "past"), ((count, inner), BF16, "past")],
        [pltpu.VMEM((block, inner), F32)] * 2, wide_up, (act_one, up_full, narrow, flags),
    )
    conv_pieces = core_stage(conv_two[:1] + list(after(tuple(conv_two[1:]), mid)), axes)
    top, low, conv_flat, top_sums, cot_sums = call(
        conv_kernel, "conv", steps + 1, ("any",) * len(conv_pieces) + (None, None, "now", None, "now", "smem"),
        [
            ((count, inner), BF16, "past"),
            ((count, inner), BF16, "past"),
            ((inner, KERNEL * inner), BF16, "any"),
            ((24, inner), F32, None),
            ((8, model), F32, None),
        ],
        [
            padded,
            pltpu.VMEM((2 * chips,) + conv_block.shape, BF16),
            pltpu.VMEM((2, inner, inner), F32),
            pltpu.VMEM((KERNEL * inner, inner), BF16),
            pltpu.VMEM((inner, KERNEL * inner), BF16),
            pltpu.VMEM((block, KERNEL * inner), BF16),
        ]
        + [pltpu.VMEM((block, inner), F32)] * 4
        + [pltpu.SemaphoreType.DMA((2 * chips + 1,))],
        wide_conv + wide_up, (*conv_pieces, mid, down_full, cotangent, narrow, flags, place),
    )
    conv_kept, conv_sent = call(
        weights_kernel, "weights", 1, (None, None, None, "smem"),
        [((dp, columns, conv_rows, inner), BF16, "any")] * 2,
        [
            padded,
            pltpu.VMEM((count, KERNEL * inner), BF16),
            pltpu.VMEM((inner, KERNEL * inner), F32),
            pltpu.VMEM((4, conv_rows, inner), F32),
            pltpu.VMEM((2, dp, columns, conv_rows, inner), BF16),
            pltpu.SemaphoreType.DMA((2,)),
        ],
        wide_conv, (low, mid, flags, place),
    )
    (output,) = call(
        output_kernel, "output", steps, (block, block, None, None),
        [((count, model), BF16, block)],
        [], wide_up, (inputs, top, down_full, after(wide, conv_sent)),
    )
    conv_grad = add_up(after(conv_kept, output), [swap(conv_sent, *axes[2], 1)])
    conv_stage = scatter_stage(conv_grad, axes[0])
    up_low, mid_sums = call(
        mid_grad_kernel, "mid_grad", steps + 1, (None, None, "past", None, "now", "past"),
        [((count, inner), BF16, "past"), ((24, inner), F32, None)],
        [
            padded,
            pltpu.VMEM((block, KERNEL * inner), BF16),
            pltpu.VMEM((block, inner), F32),
            pltpu.VMEM((block, inner), F32),
        ],
        wide_conv, (low, conv_flat, up_out, after(narrow, conv_grad), flags, flags),
    )
    up_kept, up_sent = call(
        up_weight_kernel, "up_weight", 4, ("early half", "late half", None, None, "smem"),
        [((dp, columns, 2, share, inner), BF16, "any")] * 2,
        [
            pltpu.VMEM((model // 2, inner), F32),
            pltpu.VMEM((2, dp, columns, 2, share, inner), BF16),
            pltpu.SemaphoreType.DMA((2,)),
        ],
        1, (act_one, cotangent, up_low, top, place),
    )
    conv_arrived = after(tuple(conv_stage[1]), up_kept)
    up_grad = add_up(up_kept, [swap(after(up_sent, *conv_arrived), *axes[2], 1)])
    up_stage = scatter_stage(up_grad, axes[0])
    conv_grad = add_up(conv_stage[0], conv_arrived)
    conv_stage = scatter_stage(conv_grad, axes[1])
    input_grad, small_kept, small_sent = call(
        input_grad_kernel, "input_grad", steps + 1,
        ("now", None, "past", "past", None, None, None, None, "smem"),
        [((count, model), F32, "past")] + [((dp, columns, 16, 128), F32, "any")] * 2,
        [
            pltpu.VMEM((block, model), F32),
            pltpu.VMEM((block, model), F32),
            pltpu.VMEM((16, model), F32),
            pltpu.VMEM((8, model), F32),
            pltpu.VMEM((8, inner), F32),
            pltpu.VMEM((2, dp, columns, 16, 128), F32),
            pltpu.SemaphoreType.DMA((2,)),
        ],
        wide_up,
        (up_low, up_full, inputs, cotangent, wide, top_sums, mid_sums, cot_sums, after(place, conv_grad, up_grad)),
    )
    up_arrived, conv_arrived = after((tuple(up_stage[1]), tuple(conv_stage[1])), small_kept)
    small = small_kept + swap(after(small_sent, *up_arrived, *conv_arrived), *axes[2], 1)
    up_stage = scatter_stage(add_up(up_stage[0], up_arrived), axes[1])
    small_own = exact_stage(exact_stage(small, axes[0]), axes[1])
    conv_own = add_up(conv_stage[0], conv_arrived)[0:conv_share]
    up_own, down_own = add_up(*up_stage)
    wide_row, narrow_row = up_weight.shape[0], conv_weight.shape[1]
    sums = [small_own[at, :wide_row] for at in range(2)]
    sums += [small_own[8 + at, :narrow_row] for at in range(6)]
    sums.append(small_own[2, :wide_row])
    return (output, input_grad, up_own, conv_own.reshape(conv_weight.shape), down_own.T) + tuple(sums)


def solution(mesh):
    rows, columns = mesh.shape["dp"], mesh.shape["fsdp"] // 2
    split = Mesh(mesh.devices.reshape(rows, columns, 2), ALL)
    axes = (("dp", rows), ("chip", columns), ("core", 2))
    by_row = P(ALL)
    by_second = P(None, ALL)
    in_specs = [by_row] * 16
    in_specs[10] = in_specs[14] = by_second
    out_specs = [by_row] * 14
    out_specs[3] = out_specs[4] = by_second
    return jax.shard_map(
        functools.partial(body, axes),
        mesh=split,
        in_specs=tuple(in_specs),
        out_specs=tuple(out_specs),
        check_vma=False,
    )
```

profile of v0, /device:TPU:0, one launch (start us, length us, event | category | flops | bytes accessed | tf_op | source)
XLA Modules:
  0.0 224.8 jit_solution(1966111052046899913)
XLA Ops:
  0.6 0.9 fusion.22
  1.6 4.1 %collective-permute-start.2 = (bf16[88,640]{1,0:T(8,128)(2,1)S(1)}, bf16[88,640]{1,0:T(8,128)(2,1)S(1)}, u32[]{:S(2)}, u32[]{:S(2)}) collective-permute-start(bf16[88,640]{1,0:T(8,128)(2,1)S(1)} %fusion.22), channel_id=1, source_target_pairs={{0,4},{2,6},{4,0},{6,2},{1,5},{3,7},{5,1},{7,3},{8,12},{10,14},{12... | collective-permute-start | bytes 337928 | tf_op jit(solution)/shard_map/ppermute | solution.py:24
  5.7 1.6 collective-permute-start.1
  7.3 1.0 fusion.32
  8.2 4.6 %collective-permute-done.2 = bf16[88,640]{1,0:T(8,128)(2,1)S(1)} collective-permute-done((bf16[88,640]{1,0:T(8,128)(2,1)S(1)}, bf16[88,640]{1,0:T(8,128)(2,1)S(1)}, u32[]{:S(2)}, u32[]{:S(2)}) %collective-permute-start.2) | collective-permute-done | bytes 112672 | tf_op jit(solution)/shard_map/ppermute | solution.py:24
  12.8 1.9 collective-permute-done.3
  14.9 2.5 %collective-permute-start.8 = (bf16[4,88,640]{2,1,0:T(8,128)(2,1)S(1)}, bf16[4,88,640]{2,1,0:T(8,128)(2,1)S(1)}, u32[]{:S(2)}, u32[]{:S(2)}) collective-permute-start(bf16[4,88,640]{2,1,0:T(8,128)(2,1)S(1)} %pad_maximum_fusion.2), channel_id=1, source_target_pairs={{0,24},{8,16},{16,8},{24,0},{1,25},{9,17},{17,9},{25,1},{2,26},{10... | collective-permute-start | bytes 1351688 | tf_op jit(solution)/shard_map/ppermute | solution.py:24
  18.4 0.9 reshape.253
  19.4 2.0 collective-permute-start
  21.4 3.4 %collective-permute-start.5 = (bf16[104,640]{1,0:T(8,128)(2,1)S(1)}, bf16[104,640]{1,0:T(8,128)(2,1)S(1)}, u32[]{:S(2)}, u32[]{:S(2)}) collective-permute-start(bf16[104,640]{1,0:T(8,128)(2,1)S(1)} %pad.44), channel_id=1, source_target_pairs={{0,6},{2,4},{4,2},{6,0},{1,7},{3,5},{5,3},{7,1},{8,14},{10,12},{12... | collective-permute-start | bytes 399368 | tf_op jit(solution)/shard_map/ppermute | solution.py:24
  24.8 5.0 %collective-permute-start.4 = (bf16[104,640]{1,0:T(8,128)(2,1)S(1)}, bf16[104,640]{1,0:T(8,128)(2,1)S(1)}, u32[]{:S(2)}, u32[]{:S(2)}) collective-permute-start(bf16[104,640]{1,0:T(8,128)(2,1)S(1)} %pad.44), channel_id=1, source_target_pairs={{0,4},{2,6},{4,0},{6,2},{1,5},{3,7},{5,1},{7,3},{8,12},{10,14},{12... | collective-permute-start | bytes 399368 | tf_op jit(solution)/shard_map/ppermute | solution.py:24
  29.8 0.8 reduce-window.8
  30.8 0.9 collective-permute-done.5
  31.7 3.4 %collective-permute-done.4 = bf16[104,640]{1,0:T(8,128)(2,1)S(1)} collective-permute-done((bf16[104,640]{1,0:T(8,128)(2,1)S(1)}, bf16[104,640]{1,0:T(8,128)(2,1)S(1)}, u32[]{:S(2)}, u32[]{:S(2)}) %collective-permute-start.4) | collective-permute-done | bytes 133152 | tf_op jit(solution)/shard_map/ppermute | solution.py:24
  35.1 1.6 collective-permute-done.7
  36.8 0.8 copy-done.14
  37.5 1.3 pad_maximum_fusion.own_pieces
  39.1 0.9 pad_maximum_fusion.1.refs_0_
  40.0 1.6 collective-permute-start.11
  41.6 1.3 collective-permute-start.10
  42.9 0.5 collective-permute-start.9
  44.3 2.7 %copy-done = bf16[2048,1280]{1,0:T(8,128)(2,1)S(1)} copy-done((bf16[2048,1280]{1,0:T(8,128)(2,1)S(1)}, bf16[2048,1280]{1,0:T(8,128)(2,1)}, u32[]{:S(2)}) %copy-start) | copy-done | bytes 5242904
  47.1 13.6 %first_act.1 = (bf16[2048,1280]{1,0:T(8,128)(2,1)S(1)}, bf16[1280,640]{1,0:T(8,128)(2,1)S(1)}, bf16[1280,640]{1,0:T(8,128)(2,1)S(1)}, f32[8,1280]{1,0:T(8,128)S(1)}, f32[8,640]{1,0:T(8,128)S(1)}) custom-call(bf16[4,4,88,640]{3,2,1,0:T(8,128)(2,1)S(1)} %pad_maximum_fusion.own_pieces, bf16[4,4,88,640]{3,2,1,0:T(8,128)(2,1)} %collective-permute-done.12.other_pieces, ...), custom_call_target="tpu_custom_call" | custom-call | flops 52428800 | bytes 17428492 | tf_op jit(solution)/shard_map/first_act/pallas_call | solution.py:485
  60.7 7.0 %up.1 = (f32[2048,640]{1,0:T(8,128)S(1)}, bf16[2048,640]{1,0:T(8,128)(2,1)S(1)}) custom-call(bf16[2048,1280]{1,0:T(8,128)(2,1)S(1)} %get-tuple-element.73.act_ref, bf16[1280,640]{1,0:T(8,128)(2,1)S(1)} %get-tuple-element.74.weight_ref, f32[8,640]{1,0:T(8,128)S(1)} %get-tuple-element.90.narrow_ref.refs_11_, ...), custom_call_target="tpu_custom_call" | custom-call | flops 3355443200 | bytes 14831616 | tf_op jit(solution)/shard_map/up/pallas_call | solution.py:485
  67.7 2.3 %copy-done.8 = f32[2048,640]{1,0:T(8,128)} copy-done((f32[2048,640]{1,0:T(8,128)}, f32[2048,640]{1,0:T(8,128)S(1)}, u32[]{:S(2)}) %copy-start.8) | copy-done | bytes 5242904
  70.0 1.5 copy-done.10
  72.3 1.4 collective-permute-done.14.refs_5_
  73.7 0.8 collective-permute-done.15.refs_6_
  74.5 0.8 collective-permute-done.16.refs_7_
  75.3 29.6 %conv.1 = (bf16[2048,640]{1,0:T(8,128)(2,1)S(1)}, bf16[2048,640]{1,0:T(8,128)(2,1)S(1)}, bf16[640,3200]{1,0:T(8,128)(2,1)}, f32[24,640]{1,0:T(8,128)S(1)}, f32[8,1280]{1,0:T(8,128)S(1)}) custom-call(bf16[4,104,640]{2,1,0:T(8,128)(2,1)} %pad_maximum_fusion.1.refs_0_, bf16[4,104,640]{2,1,0:T(8,128)(2,1)} %collective-permute-done.9.refs_1_, ...), custom_call_target="tpu_custom_call" | custom-call | flops 11744051200 | bytes 23289868 | tf_op jit(solution)/shard_map/conv/pallas_call | solution.py:485
  104.9 1.5 copy-done.12
  106.4 2.7 %copy-done.13 = bf16[2048,640]{1,0:T(8,128)(2,1)S(1)} copy-done((bf16[2048,640]{1,0:T(8,128)(2,1)S(1)}, bf16[2048,640]{1,0:T(8,128)(2,1)}, u32[]{:S(2)}) %copy-start.13) | copy-done | bytes 2621464
  109.2 13.1 %weights.1 = (bf16[4,4,104,640]{3,2,1,0:T(8,128)(2,1)S(1)}, bf16[4,4,104,640]{3,2,1,0:T(8,128)(2,1)S(1)}) custom-call(bf16[2048,640]{1,0:T(8,128)(2,1)S(1)} %copy-done.13, bf16[2048,640]{1,0:T(8,128)(2,1)} %copy-done.10, f32[2048,8]{1,0:T(8,128)S(1)} %concatenate.10.flags_ref.refs_12_.now_flags_ref, s32[3]{0:T(128)S(1)} %pad_add_fusion.place_ref.refs_13_), custom_call_target="tpu_custom_call" | custom-call | flops 8388608000 | bytes 9568268 | tf_op jit(solution)/shard_map/weights/pallas_call | solution.py:485
  122.5 7.0 %output.1 = bf16[2048,1280]{1,0:T(8,128)(2,1)} custom-call(bf16[2048,1280]{1,0:T(8,128)(2,1)S(1)} %bitcast.125, bf16[2048,640]{1,0:T(8,128)(2,1)S(1)} %get-tuple-element.81.top_ref, bf16[1280,640]{1,0:T(8,128)(2,1)S(1)} %get-tuple-element.80.refs_9_.weight_ref, f32[8,1280]{1,0:T(8,128)S(1)} %get-tuple-element.85.wide_ref), custom_call_target="tpu_custom_call" | custom-call | flops 3355443200 | bytes 14786560 | tf_op jit(solution)/shard_map/output/pallas_call | solution.py:485
  129.6 2.8 %fusion.26 = (bf16[4,4,104,640]{3,2,1,0:T(8,128)(2,1)S(1)}, f32[4,4,104,640]{3,2,1,0:T(8,128)}) fusion(bf16[4,4,104,640]{3,2,1,0:T(8,128)(2,1)S(1)} %collective-permute-done.17, bf16[4,4,104,640]{3,2,1,0:T(8,128)(2,1)S(1)} %get-tuple-element.89), kind=kLoop, calls=%fused_computation.85 | loop fusion | flops 4259840 | bytes 10649600 | tf_op jit(solution)/shard_map/convert.13
  132.5 1.7 collective-permute-start.20
  134.2 1.3 collective-permute-start.19
  135.5 0.5 collective-permute-start.18
  136.0 2.5 %copy-done.9 = f32[2048,640]{1,0:T(8,128)S(1)} copy-done((f32[2048,640]{1,0:T(8,128)S(1)}, f32[2048,640]{1,0:T(8,128)}, u32[]{:S(2)}) %copy-start.9) | copy-done | bytes 5242904
  138.5 17.9 %mid_grad.1 = (bf16[2048,640]{1,0:T(8,128)(2,1)S(1)}, f32[24,640]{1,0:T(8,128)S(1)}) custom-call(bf16[2048,640]{1,0:T(8,128)(2,1)S(1)} %copy-done.13, bf16[640,3200]{1,0:T(8,128)(2,1)S(1)} %copy-done.11, f32[2048,640]{1,0:T(8,128)S(1)} %copy-done.9, f32[8,640]{1,0:T(8,128)S(1)} %get-tuple-element.90.narrow_ref.refs_11_, f32[2048,8]{1,0:T(8,128)S(1)} %copy-done.7, ...), custom_call_target="tpu_custom_call" | custom-call | flops 8388608000 | bytes 14794752 | tf_op jit(solution)/shard_map/mid_grad/pallas_call | solution.py:485
  156.5 10.8 %up_weight.1 = (bf16[4,4,2,40,640]{4,3,2,1,0:T(8,128)(2,1)S(1)}, bf16[4,4,2,40,640]{4,3,2,1,0:T(8,128)(2,1)S(1)}) custom-call(bf16[2048,1280]{1,0:T(8,128)(2,1)S(1)} %bitcast.129, bf16[2048,1280]{1,0:T(8,128)(2,1)S(1)} %bitcast.127, bf16[2048,640]{1,0:T(8,128)(2,1)S(1)} %get-tuple-element.91.low_ref.up_low_ref, bf16[2048,640]{1,0:T(8,128)(2,1)S(1)} %copy-done.2, ...), custom_call_target="tpu_custom_call" | custom-call | flops 1 | bytes 1 | tf_op jit(solution)/shard_map/up_weight/pallas_call | solution.py:485
  167.4 1.5 fusion.29
  168.9 2.5 %collective-permute-start.27 = (bf16[104,640]{1,0:T(8,128)(2,1)S(1)}, bf16[104,640]{1,0:T(8,128)(2,1)S(1)}, u32[]{:S(2)}, u32[]{:S(2)}) collective-permute-start(bf16[104,640]{1,0:T(8,128)(2,1)S(1)} %get-tuple-element.131), channel_id=1, source_target_pairs={{0,6},{2,4},{4,2},{6,0},{1,7},{3,5},{5,3},{7,1},{8,14},{10,12},{12... | collective-permute-start | bytes 399368 | tf_op jit(solution)/shard_map/ppermute | solution.py:24
  171.4 2.6 %collective-permute-start.26 = (bf16[104,640]{1,0:T(8,128)(2,1)S(1)}, bf16[104,640]{1,0:T(8,128)(2,1)S(1)}, u32[]{:S(2)}, u32[]{:S(2)}) collective-permute-start(bf16[104,640]{1,0:T(8,128)(2,1)S(1)} %get-tuple-element.132), channel_id=1, source_target_pairs={{0,4},{2,6},{4,0},{6,2},{1,5},{3,7},{5,1},{7,3},{8,12},{10,14},{12... | collective-permute-start | bytes 399368 | tf_op jit(solution)/shard_map/ppermute | solution.py:24
  174.6 1.7 collective-permute-start.24
  176.3 1.3 collective-permute-start.23
  177.6 0.5 collective-permute-start.22
  178.2 4.8 %collective-permute-start.25 = (bf16[104,640]{1,0:T(8,128)(2,1)S(1)}, bf16[104,640]{1,0:T(8,128)(2,1)S(1)}, u32[]{:S(2)}, u32[]{:S(2)}) collective-permute-start(bf16[104,640]{1,0:T(8,128)(2,1)S(1)} %get-tuple-element.133), channel_id=1, source_target_pairs={{0,2},{2,0},{4,6},{6,4},{1,3},{3,1},{5,7},{7,5},{8,10},{10,8},{12,... | collective-permute-start | bytes 399368 | tf_op jit(solution)/shard_map/ppermute | solution.py:24
  183.0 19.9 %input_grad.1 = (f32[2048,1280]{1,0:T(8,128)}, f32[4,4,16,128]{3,2,1,0:T(8,128)S(1)}, f32[4,4,16,128]{3,2,1,0:T(8,128)S(1)}) custom-call(bf16[2048,640]{1,0:T(8,128)(2,1)S(1)} %get-tuple-element.91.low_ref.up_low_ref, bf16[1280,640]{1,0:T(8,128)(2,1)S(1)} %copy-done.5, bf16[2048,1280]{1,0:T(8,128)(2,1)S(1)} %bitcast.125, bf16[2048,1280]{1,0:T(8,128)(2,1)S(1)} %bitcast.127, ...), custom_call_target="tpu_custom_call" | custom-call | flops 3355443200 | bytes 25698316 | tf_op jit(solution)/shard_map/input_grad/pallas_call | solution.py:485
  203.2 0.7 reshape.256
  204.2 2.4 %collective-permute-start.30 = (bf16[2,40,640]{2,1,0:T(8,128)(2,1)S(1)}, bf16[2,40,640]{2,1,0:T(8,128)(2,1)S(1)}, u32[]{:S(2)}, u32[]{:S(2)}) collective-permute-start(bf16[2,40,640]{2,1,0:T(8,128)(2,1)S(1)} %get-tuple-element.135), channel_id=1, source_target_pairs={{0,6},{2,4},{4,2},{6,0},{1,7},{3,5},{5,3},{7,1},{8,14},{10,12},{12... | collective-permute-start | bytes 307208 | tf_op jit(solution)/shard_map/ppermute | solution.py:24
  206.6 1.0 collective-permute-start.29
  207.6 1.5 collective-permute-start.33
  209.1 1.5 collective-permute-start.34
  210.6 0.5 collective-permute-start.32
  211.1 1.4 collective-permute-done.30
  212.6 4.5 %collective-permute-done.29 = bf16[2,40,640]{2,1,0:T(8,128)(2,1)S(1)} collective-permute-done((bf16[2,40,640]{2,1,0:T(8,128)(2,1)S(1)}, bf16[2,40,640]{2,1,0:T(8,128)(2,1)S(1)}, u32[]{:S(2)}, u32[]{:S(2)}) %collective-permute-start.29) | collective-permute-done | bytes 102432 | tf_op jit(solution)/shard_map/ppermute | solution.py:24
  217.3 2.5 %collective-permute-start.37 = (f32[16,128]{1,0:T(8,128)S(1)}, f32[16,128]{1,0:T(8,128)S(1)}, u32[]{:S(2)}, u32[]{:S(2)}) collective-permute-start(f32[16,128]{1,0:T(8,128)S(1)} %get-tuple-element.143), channel_id=1, source_target_pairs={{0,6},{2,4},{4,2},{6,0},{1,7},{3,5},{5,3},{7,1},{8,14},{10,12},{12... | collective-permute-start | bytes 24584 | tf_op jit(solution)/shard_map/ppermute | solution.py:24
  219.8 1.0 collective-permute-start.35
  220.8 0.7 slice_bitcast_fusion.13
  221.8 1.0 collective-permute-done.37
  222.8 0.6 collective-permute-done.35
  223.5 0.5 slice_bitcast_fusion.26
  224.0 0.5 slice_bitcast_fusion.27
  (118 shorter events, 5.4 us)
Async XLA Ops:
  1.6 11.3 %collective-permute-start.2 = (bf16[88,640]{1,0:T(8,128)(2,1)S(1)}, bf16[88,640]{1,0:T(8,128)(2,1)S(1)}, u32[]{:S(2)}, u32[]{:S(2)}) collective-permute-start(bf16[88,640]{1,0:T(8,128)(2,1)S(1)} %fusion.22), channel_id=1, source_target_pairs={{0,4},{2,6},{4,0},{6,2},{1,5},{3,7},{5,1},{7,3},{8,12},{10,14},{12... | collective-permute-start | bytes 337928 | tf_op jit(solution)/shard_map/ppermute | solution.py:24
  5.7 7.2 %collective-permute-start.1 = (bf16[88,640]{1,0:T(8,128)(2,1)S(1)}, bf16[88,640]{1,0:T(8,128)(2,1)S(1)}, u32[]{:S(2)}, u32[]{:S(2)}) collective-permute-start(bf16[88,640]{1,0:T(8,128)(2,1)S(1)} %fusion.22), channel_id=1, source_target_pairs={{0,2},{2,0},{4,6},{6,4},{1,3},{3,1},{5,7},{7,5},{8,10},{10,8},{12,... | collective-permute-start | bytes 337928 | tf_op jit(solution)/shard_map/ppermute | solution.py:24
  7.3 7.5 %collective-permute-start.3 = (bf16[88,640]{1,0:T(8,128)(2,1)S(1)}, bf16[88,640]{1,0:T(8,128)(2,1)S(1)}, u32[]{:S(2)}, u32[]{:S(2)}) collective-permute-start(bf16[88,640]{1,0:T(8,128)(2,1)S(1)} %fusion.22), channel_id=1, source_target_pairs={{0,6},{2,4},{4,2},{6,0},{1,7},{3,5},{5,3},{7,1},{8,14},{10,12},{12... | collective-permute-start | bytes 337928 | tf_op jit(solution)/shard_map/ppermute | solution.py:24
  14.8 24.2 %copy-start.19 = (s32[2048]{0:T(1024)S(1)}, s32[2048]{0:T(1024)}, u32[]{:S(2)}) copy-start(s32[2048]{0:T(1024)} %param.18) | copy-start | bytes 24580
  14.9 20.2 %collective-permute-start.8 = (bf16[4,88,640]{2,1,0:T(8,128)(2,1)S(1)}, bf16[4,88,640]{2,1,0:T(8,128)(2,1)S(1)}, u32[]{:S(2)}, u32[]{:S(2)}) collective-permute-start(bf16[4,88,640]{2,1,0:T(8,128)(2,1)S(1)} %pad_maximum_fusion.2), channel_id=1, source_target_pairs={{0,24},{8,16},{16,8},{24,0},{1,25},{9,17},{17,9},{25,1},{2,26},{10... | collective-permute-start | bytes 1351688 | tf_op jit(solution)/shard_map/ppermute | solution.py:24
  17.4 19.3 %collective-permute-start.7 = (bf16[4,88,640]{2,1,0:T(8,128)(2,1)S(1)}, bf16[4,88,640]{2,1,0:T(8,128)(2,1)S(1)}, u32[]{:S(2)}, u32[]{:S(2)}) collective-permute-start(bf16[4,88,640]{2,1,0:T(8,128)(2,1)S(1)} %pad_maximum_fusion.2), channel_id=1, source_target_pairs={{0,16},{8,24},{16,0},{24,8},{1,17},{9,25},{17,1},{25,9},{2,18},{10... | collective-permute-start | bytes 1351688 | tf_op jit(solution)/shard_map/ppermute | solution.py:24
  17.9 18.9 %collective-permute-start.6 = (bf16[4,88,640]{2,1,0:T(8,128)(2,1)S(1)}, bf16[4,88,640]{2,1,0:T(8,128)(2,1)S(1)}, u32[]{:S(2)}, u32[]{:S(2)}) collective-permute-start(bf16[4,88,640]{2,1,0:T(8,128)(2,1)S(1)} %pad_maximum_fusion.2), channel_id=1, source_target_pairs={{0,8},{8,0},{16,24},{24,16},{1,9},{9,1},{17,25},{25,17},{2,10},{10... | collective-permute-start | bytes 1351688 | tf_op jit(solution)/shard_map/ppermute | solution.py:24
  19.4 5.4 %collective-permute-start = (bf16[104,640]{1,0:T(8,128)(2,1)S(1)}, bf16[104,640]{1,0:T(8,128)(2,1)S(1)}, u32[]{:S(2)}, u32[]{:S(2)}) collective-permute-start(bf16[104,640]{1,0:T(8,128)(2,1)S(1)} %pad.44), channel_id=1, source_target_pairs={{0,2},{2,0},{4,6},{6,4},{1,3},{3,1},{5,7},{7,5},{8,10},{10,8},{12,... | collective-permute-start | bytes 399368 | tf_op jit(solution)/shard_map/ppermute | solution.py:24
  21.4 10.3 %collective-permute-start.5 = (bf16[104,640]{1,0:T(8,128)(2,1)S(1)}, bf16[104,640]{1,0:T(8,128)(2,1)S(1)}, u32[]{:S(2)}, u32[]{:S(2)}) collective-permute-start(bf16[104,640]{1,0:T(8,128)(2,1)S(1)} %pad.44), channel_id=1, source_target_pairs={{0,6},{2,4},{4,2},{6,0},{1,7},{3,5},{5,3},{7,1},{8,14},{10,12},{12... | collective-permute-start | bytes 399368 | tf_op jit(solution)/shard_map/ppermute | solution.py:24
  24.8 10.3 %collective-permute-start.4 = (bf16[104,640]{1,0:T(8,128)(2,1)S(1)}, bf16[104,640]{1,0:T(8,128)(2,1)S(1)}, u32[]{:S(2)}, u32[]{:S(2)}) collective-permute-start(bf16[104,640]{1,0:T(8,128)(2,1)S(1)} %pad.44), channel_id=1, source_target_pairs={{0,4},{2,6},{4,0},{6,2},{1,5},{3,7},{5,1},{7,3},{8,12},{10,14},{12... | collective-permute-start | bytes 399368 | tf_op jit(solution)/shard_map/ppermute | solution.py:24
  31.7 5.1 %copy-start.15 = (bf16[104,640]{1,0:T(8,128)(2,1)}, bf16[104,640]{1,0:T(8,128)(2,1)S(1)}, u32[]{:S(2)}) copy-start(bf16[104,640]{1,0:T(8,128)(2,1)S(1)} %collective-permute-done.5) | copy-start | bytes 399364
  35.1 1.7 copy-start.17
  36.8 0.8 copy-start.14
  37.5 1.5 copy-start.16
  37.5 1.5 copy-start.18
  38.9 5.4 %collective-permute-start.12 = (bf16[4,4,88,640]{3,2,1,0:T(8,128)(2,1)S(1)}, bf16[4,4,88,640]{3,2,1,0:T(8,128)(2,1)}, u32[]{:S(2)}, u32[]{:S(2)}) collective-permute-start(bf16[4,4,88,640]{3,2,1,0:T(8,128)(2,1)S(1)} %pad_maximum_fusion.own_pieces), channel_id=1, source_target_pairs={{0,1},{1,0},{2,3},{3,2},{4,5},{5,4},{6,7},{7,6},{8,9},{9,8},{10,11... | collective-permute-start | bytes 5406728 | tf_op jit(solution)/shard_map/ppermute | solution.py:24
  40.0 31.5 %collective-permute-start.11 = (bf16[4,104,640]{2,1,0:T(8,128)(2,1)}, bf16[4,104,640]{2,1,0:T(8,128)(2,1)}, u32[]{:S(2)}, u32[]{:S(2)}) collective-permute-start(bf16[4,104,640]{2,1,0:T(8,128)(2,1)} %pad_maximum_fusion.1.refs_0_), channel_id=1, source_target_pairs={{0,24},{8,16},{16,8},{24,0},{1,25},{9,17},{17,9},{25,1},{2,26},{10... | collective-permute-start | bytes 1597448 | tf_op jit(solution)/shard_map/ppermute | solution.py:24
  41.6 29.9 %collective-permute-start.10 = (bf16[4,104,640]{2,1,0:T(8,128)(2,1)}, bf16[4,104,640]{2,1,0:T(8,128)(2,1)}, u32[]{:S(2)}, u32[]{:S(2)}) collective-permute-start(bf16[4,104,640]{2,1,0:T(8,128)(2,1)} %pad_maximum_fusion.1.refs_0_), channel_id=1, source_target_pairs={{0,16},{8,24},{16,0},{24,8},{1,17},{9,25},{17,1},{25,9},{2,18},{10... | collective-permute-start | bytes 1597448 | tf_op jit(solution)/shard_map/ppermute | solution.py:24
  42.9 28.6 %collective-permute-start.9 = (bf16[4,104,640]{2,1,0:T(8,128)(2,1)}, bf16[4,104,640]{2,1,0:T(8,128)(2,1)}, u32[]{:S(2)}, u32[]{:S(2)}) collective-permute-start(bf16[4,104,640]{2,1,0:T(8,128)(2,1)} %pad_maximum_fusion.1.refs_0_), channel_id=1, source_target_pairs={{0,8},{8,0},{16,24},{24,16},{1,9},{9,1},{17,25},{25,17},{2,10},{10... | collective-permute-start | bytes 1597448 | tf_op jit(solution)/shard_map/ppermute | solution.py:24
  44.2 62.2 %copy-start.6 = (f32[2048,8]{1,0:T(8,128)}, f32[2048,8]{1,0:T(8,128)S(1)}, u32[]{:S(2)}) copy-start(f32[2048,8]{1,0:T(8,128)S(1)} %concatenate.10.flags_ref.refs_12_.now_flags_ref) | copy-start | bytes 196612
  44.3 28.1 %collective-permute-start.13 = (bf16[4,104,640]{2,1,0:T(8,128)(2,1)}, bf16[4,104,640]{2,1,0:T(8,128)(2,1)S(1)}, u32[]{:S(2)}, u32[]{:S(2)}) collective-permute-start(bf16[4,104,640]{2,1,0:T(8,128)(2,1)} %pad_maximum_fusion.1.refs_0_), channel_id=1, source_target_pairs={{0,1},{1,0},{2,3},{3,2},{4,5},{5,4},{6,7},{7,6},{8,9},{9,8},{10,11... | collective-permute-start | bytes 1597448 | tf_op jit(solution)/shard_map/ppermute | solution.py:24
  44.3 2.8 %copy-start = (bf16[2048,1280]{1,0:T(8,128)(2,1)S(1)}, bf16[2048,1280]{1,0:T(8,128)(2,1)}, u32[]{:S(2)}) copy-start(bf16[2048,1280]{1,0:T(8,128)(2,1)} %x_ref.5) | copy-start | bytes 15728644
  60.6 7.0 %copy-start.3 = (bf16[2048,1280]{1,0:T(8,128)(2,1)}, bf16[2048,1280]{1,0:T(8,128)(2,1)S(1)}, u32[]{:S(2)}) copy-start(bf16[2048,1280]{1,0:T(8,128)(2,1)S(1)} %get-tuple-element.73.act_ref) | copy-start | bytes 15728644
  60.7 7.0 %copy-start.4 = (bf16[1280,640]{1,0:T(8,128)(2,1)}, bf16[1280,640]{1,0:T(8,128)(2,1)S(1)}, u32[]{:S(2)}) copy-start(bf16[1280,640]{1,0:T(8,128)(2,1)S(1)} %get-tuple-element.74.weight_ref) | copy-start | bytes 4915204
  67.7 2.4 %copy-start.8 = (f32[2048,640]{1,0:T(8,128)}, f32[2048,640]{1,0:T(8,128)S(1)}, u32[]{:S(2)}) copy-start(f32[2048,640]{1,0:T(8,128)S(1)} %get-tuple-element.87.up_out_ref) | copy-start | bytes 15728644
  70.0 1.5 copy-start.10
  71.5 2.2 collective-permute-start.14
  71.8 2.7 %collective-permute-start.15 = (bf16[4,104,640]{2,1,0:T(8,128)(2,1)}, bf16[4,104,640]{2,1,0:T(8,128)(2,1)S(1)}, u32[]{:S(2)}, u32[]{:S(2)}) collective-permute-start(bf16[4,104,640]{2,1,0:T(8,128)(2,1)} %collective-permute-done.10.refs_2_), channel_id=1, source_target_pairs={{0,1},{1,0},{2,3},{3,2},{4,5},{5,4},{6,7},{7,6},{8,9},{9,8},{10,11... | collective-permute-start | bytes 1597448 | tf_op jit(solution)/shard_map/ppermute | solution.py:24
  72.1 3.1 %collective-permute-start.16 = (bf16[4,104,640]{2,1,0:T(8,128)(2,1)}, bf16[4,104,640]{2,1,0:T(8,128)(2,1)S(1)}, u32[]{:S(2)}, u32[]{:S(2)}) collective-permute-start(bf16[4,104,640]{2,1,0:T(8,128)(2,1)} %collective-permute-done.11.refs_3_), channel_id=1, source_target_pairs={{0,1},{1,0},{2,3},{3,2},{4,5},{5,4},{6,7},{7,6},{8,9},{9,8},{10,11... | collective-permute-start | bytes 1597448 | tf_op jit(solution)/shard_map/ppermute | solution.py:24
  104.8 1.6 copy-start.12
  106.4 16.1 %copy-start.1 = (bf16[2048,640]{1,0:T(8,128)(2,1)}, bf16[2048,640]{1,0:T(8,128)(2,1)S(1)}, u32[]{:S(2)}) copy-start(bf16[2048,640]{1,0:T(8,128)(2,1)S(1)} %get-tuple-element.81.top_ref) | copy-start | bytes 7864324
  106.4 16.1 %slice-start = ((s8[5242880]{0:T(1024)(128)(4,1)}), s8[4194304]{0:T(1024)(128)(4,1)S(1)}, s32[]{:S(2)}) async-start(s8[5242880]{0:T(1024)(128)(4,1)} %bitcast.124), calls=%async_computation | async-start | bytes 8388608
  106.4 2.7 %copy-start.13 = (bf16[2048,640]{1,0:T(8,128)(2,1)S(1)}, bf16[2048,640]{1,0:T(8,128)(2,1)}, u32[]{:S(2)}) copy-start(bf16[2048,640]{1,0:T(8,128)(2,1)} %copy-done.12) | copy-start | bytes 7864324
  109.2 13.4 %slice-start.1 = ((s8[5242880]{0:T(1024)(128)(4,1)}), s8[1048576]{0:T(1024)(128)(4,1)S(1)}, s32[]{:S(2)}) async-start(s8[5242880]{0:T(1024)(128)(4,1)} %bitcast.124), calls=%async_computation.1 | async-start | bytes 2097152
  122.2 7.3 %collective-permute-start.17 = (bf16[4,4,104,640]{3,2,1,0:T(8,128)(2,1)S(1)}, bf16[4,4,104,640]{3,2,1,0:T(8,128)(2,1)S(1)}, u32[]{:S(2)}, u32[]{:S(2)}) collective-permute-start(bf16[4,4,104,640]{3,2,1,0:T(8,128)(2,1)S(1)} %get-tuple-element.84), channel_id=1, source_target_pairs={{0,1},{1,0},{2,3},{3,2},{4,5},{5,4},{6,7},{7,6},{8,9},{9,8},{10,11... | collective-permute-start | bytes 6389768 | tf_op jit(solution)/shard_map/ppermute | solution.py:24
  129.6 6.5 %copy-start.11 = (bf16[640,3200]{1,0:T(8,128)(2,1)S(1)}, bf16[640,3200]{1,0:T(8,128)(2,1)}, u32[]{:S(2)}) copy-start(bf16[640,3200]{1,0:T(8,128)(2,1)} %get-tuple-element.86.flat_ref) | copy-start | bytes 12288004
  132.3 3.7 %copy-start.7 = (f32[2048,8]{1,0:T(8,128)S(1)}, f32[2048,8]{1,0:T(8,128)}, u32[]{:S(2)}) copy-start(f32[2048,8]{1,0:T(8,128)} %copy-done.6) | copy-start | bytes 196612
  132.3 24.1 %slice-start.2 = ((s8[5242880]{0:T(1024)(128)(4,1)}), s8[4194304]{0:T(1024)(128)(4,1)S(1)}, s32[]{:S(2)}) async-start(s8[5242880]{0:T(1024)(128)(4,1)} %bitcast.126), calls=%async_computation.2 | async-start | bytes 8388608
  132.3 24.1 %slice-start.4 = ((s8[5242880]{0:T(1024)(128)(4,1)}), s8[4194304]{0:T(1024)(128)(4,1)S(1)}, s32[]{:S(2)}) async-start(s8[5242880]{0:T(1024)(128)(4,1)} %bitcast.128), calls=%async_computation.4 | async-start | bytes 8388608
  132.5 34.8 %collective-permute-start.20 = (bf16[4,104,640]{2,1,0:T(8,128)(2,1)S(1)}, bf16[4,104,640]{2,1,0:T(8,128)(2,1)S(1)}, u32[]{:S(2)}, u32[]{:S(2)}) collective-permute-start(bf16[4,104,640]{2,1,0:T(8,128)(2,1)S(1)} %get-tuple-element.125), channel_id=1, source_target_pairs={{0,24},{8,16},{16,8},{24,0},{1,25},{9,17},{17,9},{25,1},{2,26},{10... | collective-permute-start | bytes 1597448 | tf_op jit(solution)/shard_map/ppermute | solution.py:24
  134.2 33.1 %collective-permute-start.19 = (bf16[4,104,640]{2,1,0:T(8,128)(2,1)S(1)}, bf16[4,104,640]{2,1,0:T(8,128)(2,1)S(1)}, u32[]{:S(2)}, u32[]{:S(2)}) collective-permute-start(bf16[4,104,640]{2,1,0:T(8,128)(2,1)S(1)} %get-tuple-element.126), channel_id=1, source_target_pairs={{0,16},{8,24},{16,0},{24,8},{1,17},{9,25},{17,1},{25,9},{2,18},{10... | collective-permute-start | bytes 1597448 | tf_op jit(solution)/shard_map/ppermute | solution.py:24
  135.5 31.8 %collective-permute-start.18 = (bf16[4,104,640]{2,1,0:T(8,128)(2,1)S(1)}, bf16[4,104,640]{2,1,0:T(8,128)(2,1)S(1)}, u32[]{:S(2)}, u32[]{:S(2)}) collective-permute-start(bf16[4,104,640]{2,1,0:T(8,128)(2,1)S(1)} %get-tuple-element.127), channel_id=1, source_target_pairs={{0,8},{8,0},{16,24},{24,16},{1,9},{9,1},{17,25},{25,17},{2,10},{10... | collective-permute-start | bytes 1597448 | tf_op jit(solution)/shard_map/ppermute | solution.py:24
  136.0 2.5 %copy-start.9 = (f32[2048,640]{1,0:T(8,128)S(1)}, f32[2048,640]{1,0:T(8,128)}, u32[]{:S(2)}) copy-start(f32[2048,640]{1,0:T(8,128)} %copy-done.8) | copy-start | bytes 15728644
  138.5 17.9 %slice-start.3 = ((s8[5242880]{0:T(1024)(128)(4,1)}), s8[1048576]{0:T(1024)(128)(4,1)S(1)}, s32[]{:S(2)}) async-start(s8[5242880]{0:T(1024)(128)(4,1)} %bitcast.126), calls=%async_computation.3 | async-start | bytes 2097152
  138.5 17.9 %copy-start.2 = (bf16[2048,640]{1,0:T(8,128)(2,1)S(1)}, bf16[2048,640]{1,0:T(8,128)(2,1)}, u32[]{:S(2)}) copy-start(bf16[2048,640]{1,0:T(8,128)(2,1)} %copy-done.1) | copy-start | bytes 7864324
  138.5 17.9 %slice-start.5 = ((s8[5242880]{0:T(1024)(128)(4,1)}), s8[1048576]{0:T(1024)(128)(4,1)S(1)}, s32[]{:S(2)}) async-start(s8[5242880]{0:T(1024)(128)(4,1)} %bitcast.128), calls=%async_computation.5 | async-start | bytes 2097152
  167.3 6.7 %collective-permute-start.21 = (bf16[4,4,2,40,640]{4,3,2,1,0:T(8,128)(2,1)S(1)}, bf16[4,4,2,40,640]{4,3,2,1,0:T(8,128)(2,1)S(1)}, u32[]{:S(2)}, u32[]{:S(2)}) collective-permute-start(bf16[4,4,2,40,640]{4,3,2,1,0:T(8,128)(2,1)S(1)} %get-tuple-element.100), channel_id=1, source_target_pairs={{0,1},{1,0},{2,3},{3,2},{4,5},{5,4},{6,7},{7,6},{8,9},{9,8},{10,11... | collective-permute-start | bytes 4915208 | tf_op jit(solution)/shard_map/ppermute | solution.py:24
  168.9 9.3 %collective-permute-start.27 = (bf16[104,640]{1,0:T(8,128)(2,1)S(1)}, bf16[104,640]{1,0:T(8,128)(2,1)S(1)}, u32[]{:S(2)}, u32[]{:S(2)}) collective-permute-start(bf16[104,640]{1,0:T(8,128)(2,1)S(1)} %get-tuple-element.131), channel_id=1, source_target_pairs={{0,6},{2,4},{4,2},{6,0},{1,7},{3,5},{5,3},{7,1},{8,14},{10,12},{12... | collective-permute-start | bytes 399368 | tf_op jit(solution)/shard_map/ppermute | solution.py:24
  171.4 31.5 %collective-permute-start.26 = (bf16[104,640]{1,0:T(8,128)(2,1)S(1)}, bf16[104,640]{1,0:T(8,128)(2,1)S(1)}, u32[]{:S(2)}, u32[]{:S(2)}) collective-permute-start(bf16[104,640]{1,0:T(8,128)(2,1)S(1)} %get-tuple-element.132), channel_id=1, source_target_pairs={{0,4},{2,6},{4,0},{6,2},{1,5},{3,7},{5,1},{7,3},{8,12},{10,14},{12... | collective-permute-start | bytes 399368 | tf_op jit(solution)/shard_map/ppermute | solution.py:24
  174.5 8.5 %copy-start.5 = (bf16[1280,640]{1,0:T(8,128)(2,1)S(1)}, bf16[1280,640]{1,0:T(8,128)(2,1)}, u32[]{:S(2)}) copy-start(bf16[1280,640]{1,0:T(8,128)(2,1)} %copy-done.4) | copy-start | bytes 4915204
  174.6 28.3 %collective-permute-start.24 = (bf16[4,2,40,640]{3,2,1,0:T(8,128)(2,1)S(1)}, bf16[4,2,40,640]{3,2,1,0:T(8,128)(2,1)S(1)}, u32[]{:S(2)}, u32[]{:S(2)}) collective-permute-start(bf16[4,2,40,640]{3,2,1,0:T(8,128)(2,1)S(1)} %get-tuple-element.128), channel_id=1, source_target_pairs={{0,24},{8,16},{16,8},{24,0},{1,25},{9,17},{17,9},{25,1},{2,26},{10... | collective-permute-start | bytes 1228808 | tf_op jit(solution)/shard_map/ppermute | solution.py:24
  176.3 26.6 %collective-permute-start.23 = (bf16[4,2,40,640]{3,2,1,0:T(8,128)(2,1)S(1)}, bf16[4,2,40,640]{3,2,1,0:T(8,128)(2,1)S(1)}, u32[]{:S(2)}, u32[]{:S(2)}) collective-permute-start(bf16[4,2,40,640]{3,2,1,0:T(8,128)(2,1)S(1)} %get-tuple-element.129), channel_id=1, source_target_pairs={{0,16},{8,24},{16,0},{24,8},{1,17},{9,25},{17,1},{25,9},{2,18},{10... | collective-permute-start | bytes 1228808 | tf_op jit(solution)/shard_map/ppermute | solution.py:24
  177.6 25.3 %collective-permute-start.22 = (bf16[4,2,40,640]{3,2,1,0:T(8,128)(2,1)S(1)}, bf16[4,2,40,640]{3,2,1,0:T(8,128)(2,1)S(1)}, u32[]{:S(2)}, u32[]{:S(2)}) collective-permute-start(bf16[4,2,40,640]{3,2,1,0:T(8,128)(2,1)S(1)} %get-tuple-element.130), channel_id=1, source_target_pairs={{0,8},{8,0},{16,24},{24,16},{1,9},{9,1},{17,25},{25,17},{2,10},{10... | collective-permute-start | bytes 1228808 | tf_op jit(solution)/shard_map/ppermute | solution.py:24
  178.2 24.7 %collective-permute-start.25 = (bf16[104,640]{1,0:T(8,128)(2,1)S(1)}, bf16[104,640]{1,0:T(8,128)(2,1)S(1)}, u32[]{:S(2)}, u32[]{:S(2)}) collective-permute-start(bf16[104,640]{1,0:T(8,128)(2,1)S(1)} %get-tuple-element.133), channel_id=1, source_target_pairs={{0,2},{2,0},{4,6},{6,4},{1,3},{3,1},{5,7},{7,5},{8,10},{10,8},{12,... | collective-permute-start | bytes 399368 | tf_op jit(solution)/shard_map/ppermute | solution.py:24
  204.0 3.6 %collective-permute-start.31 = (f32[4,4,16,128]{3,2,1,0:T(8,128)S(1)}, f32[4,4,16,128]{3,2,1,0:T(8,128)S(1)}, u32[]{:S(2)}, u32[]{:S(2)}) collective-permute-start(f32[4,4,16,128]{3,2,1,0:T(8,128)S(1)} %get-tuple-element.111), channel_id=1, source_target_pairs={{0,1},{1,0},{2,3},{3,2},{4,5},{5,4},{6,7},{7,6},{8,9},{9,8},{10,11... | collective-permute-start | bytes 393224 | tf_op jit(solution)/shard_map/ppermute | solution.py:24
  204.0 6.6 %collective-permute-start.28 = (bf16[2,40,640]{2,1,0:T(8,128)(2,1)S(1)}, bf16[2,40,640]{2,1,0:T(8,128)(2,1)S(1)}, u32[]{:S(2)}, u32[]{:S(2)}) collective-permute-start(bf16[2,40,640]{2,1,0:T(8,128)(2,1)S(1)} %get-tuple-element.134), channel_id=1, source_target_pairs={{0,2},{2,0},{4,6},{6,4},{1,3},{3,1},{5,7},{7,5},{8,10},{10,8},{12,... | collective-permute-start | bytes 307208 | tf_op jit(solution)/shard_map/ppermute | solution.py:24
  204.2 8.4 %collective-permute-start.30 = (bf16[2,40,640]{2,1,0:T(8,128)(2,1)S(1)}, bf16[2,40,640]{2,1,0:T(8,128)(2,1)S(1)}, u32[]{:S(2)}, u32[]{:S(2)}) collective-permute-start(bf16[2,40,640]{2,1,0:T(8,128)(2,1)S(1)} %get-tuple-element.135), channel_id=1, source_target_pairs={{0,6},{2,4},{4,2},{6,0},{1,7},{3,5},{5,3},{7,1},{8,14},{10,12},{12... | collective-permute-start | bytes 307208 | tf_op jit(solution)/shard_map/ppermute | solution.py:24
  206.6 10.5 %collective-permute-start.29 = (bf16[2,40,640]{2,1,0:T(8,128)(2,1)S(1)}, bf16[2,40,640]{2,1,0:T(8,128)(2,1)S(1)}, u32[]{:S(2)}, u32[]{:S(2)}) collective-permute-start(bf16[2,40,640]{2,1,0:T(8,128)(2,1)S(1)} %get-tuple-element.136), channel_id=1, source_target_pairs={{0,4},{2,6},{4,0},{6,2},{1,5},{3,7},{5,1},{7,3},{8,12},{10,14},{12... | collective-permute-start | bytes 307208 | tf_op jit(solution)/shard_map/ppermute | solution.py:24
  207.6 9.6 %collective-permute-start.33 = (f32[4,16,128]{2,1,0:T(8,128)S(1)}, f32[4,16,128]{2,1,0:T(8,128)S(1)}, u32[]{:S(2)}, u32[]{:S(2)}) collective-permute-start(f32[4,16,128]{2,1,0:T(8,128)S(1)} %get-tuple-element.139), channel_id=1, source_target_pairs={{0,16},{8,24},{16,0},{24,8},{1,17},{9,25},{17,1},{25,9},{2,18},{10... | collective-permute-start | bytes 98312 | tf_op jit(solution)/shard_map/ppermute | solution.py:24
  209.1 8.1 %collective-permute-start.34 = (f32[4,16,128]{2,1,0:T(8,128)S(1)}, f32[4,16,128]{2,1,0:T(8,128)S(1)}, u32[]{:S(2)}, u32[]{:S(2)}) collective-permute-start(f32[4,16,128]{2,1,0:T(8,128)S(1)} %get-tuple-element.140), channel_id=1, source_target_pairs={{0,24},{8,16},{16,8},{24,0},{1,25},{9,17},{17,9},{25,1},{2,26},{10... | collective-permute-start | bytes 98312 | tf_op jit(solution)/shard_map/ppermute | solution.py:24
  210.6 6.6 %collective-permute-start.32 = (f32[4,16,128]{2,1,0:T(8,128)S(1)}, f32[4,16,128]{2,1,0:T(8,128)S(1)}, u32[]{:S(2)}, u32[]{:S(2)}) collective-permute-start(f32[4,16,128]{2,1,0:T(8,128)S(1)} %get-tuple-element.141), channel_id=1, source_target_pairs={{0,8},{8,0},{16,24},{24,16},{1,9},{9,1},{17,25},{25,17},{2,10},{10... | collective-permute-start | bytes 98312 | tf_op jit(solution)/shard_map/ppermute | solution.py:24
  217.2 4.6 %collective-permute-start.36 = (f32[16,128]{1,0:T(8,128)S(1)}, f32[16,128]{1,0:T(8,128)S(1)}, u32[]{:S(2)}, u32[]{:S(2)}) collective-permute-start(f32[16,128]{1,0:T(8,128)S(1)} %get-tuple-element.142), channel_id=1, source_target_pairs={{0,4},{2,6},{4,0},{6,2},{1,5},{3,7},{5,1},{7,3},{8,12},{10,14},{12... | collective-permute-start | bytes 24584 | tf_op jit(solution)/shard_map/ppermute | solution.py:24
  217.3 5.5 %collective-permute-start.37 = (f32[16,128]{1,0:T(8,128)S(1)}, f32[16,128]{1,0:T(8,128)S(1)}, u32[]{:S(2)}, u32[]{:S(2)}) collective-permute-start(f32[16,128]{1,0:T(8,128)S(1)} %get-tuple-element.143), channel_id=1, source_target_pairs={{0,6},{2,4},{4,2},{6,0},{1,7},{3,5},{5,3},{7,1},{8,14},{10,12},{12... | collective-permute-start | bytes 24584 | tf_op jit(solution)/shard_map/ppermute | solution.py:24
  219.8 3.7 %collective-permute-start.35 = (f32[16,128]{1,0:T(8,128)S(1)}, f32[16,128]{1,0:T(8,128)S(1)}, u32[]{:S(2)}, u32[]{:S(2)}) collective-permute-start(f32[16,128]{1,0:T(8,128)S(1)} %get-tuple-element.144), channel_id=1, source_target_pairs={{0,2},{2,0},{4,6},{6,4},{1,3},{3,1},{5,7},{7,5},{8,10},{10,8},{12,... | collective-permute-start | bytes 24584 | tf_op jit(solution)/shard_map/ppermute | solution.py:24
where the time goes:
time: 228 us; the launch traced here: 225 us
  Pallas kernels  119 us (52%)
  starting transfers between devices  52.1 us (23%)
  waiting for transfers between devices  23.4 us (10%)
  local copies, waits for them, and re-layouts  18.6 us (8%)
  other arithmetic  10.5 us (5%)
    pallas_call x8, Pallas kernels, call(): pl.pallas_call(kernel, name=name, grid=(grid,), in_specs=[spec(a.shape, r...  119 us
    ppermute x38, starting transfers between devices, swap(): return lax.ppermute(array, axis, [(k, k ^ mask) for k in range(size)])  52.1 us
    ppermute x38, waiting for transfers between devices, swap(): return lax.ppermute(array, axis, [(k, k ^ mask) for k in range(size)])  23.4 us
    unnamed x52, local copies, waits for them, and re-layouts  14.2 us
    another operation x5, other arithmetic  5.78 us
  transfers between devices with their start and end apart: 38, of which 14 were waited for; matrix products, arithmetic and copies ran while one was open for 3% of the time, Pallas kernels for 34%

commit v1 on v0

--- a/solution.py
+++ b/solution.py
@@ -17,7 +17,7 @@
 TANH_ONE = 0.7978845608028654
 TANH_THREE = TANH_ONE * 0.044715
 ROWS = 32
-VMEM_MIB = {"first_act": 24, "up": 14, "conv": 40, "weights": 44, "mid_grad": 24, "up_weight": 30, "input_grad": 20, "output": 12}
+VMEM_MIB = {"first_act": 61, "up": 61, "conv": 61, "weights": 44, "mid_grad": 24, "up_weight": 30, "input_grad": 20, "output": 12}
 
 
 def swap(array, axis, size, mask):
@@ -101,14 +101,6 @@
 
 def fold(value):
     return sum(value[k : k + 8] for k in range(0, value.shape[0], 8))
-
-
-def chunks(count, body, unroll=4):
-    def step(k, carry):
-        body(pl.multiple_of(k * ROWS, ROWS))
-        return carry
-
-    lax.fori_loop(0, count // ROWS, step, 0, unroll=unroll)
 
 
 def dot(left, right, left_dim=1, right_dim=0):
@@ -130,11 +122,13 @@
     return copies
 
 
-def first_act_kernel(
-    own_pieces, other_pieces, x_ref, place_ref,
-    act_ref, up_ref, down_ref, wide_ref, narrow_ref, hold_ref, up_wide_ref, down_wide_ref, semaphores,
+def up_kernel(
+    own_pieces, other_pieces, x_ref, flags_ref, place_ref,
+    act_ref, up_ref, down_ref, wide_ref, narrow_ref, out_ref, mid_ref,
+    hold_ref, up_wide_ref, down_wide_ref, z_ref, next_ref, semaphores,
 ):
     block, width = x_ref.shape
+    inner = z_ref.shape[1]
 
     @pl.when(pl.program_id(0) == 0)
     def _():
@@ -156,21 +150,14 @@
         up_ref[...] = up_wide_ref[...].astype(BF16)
         down_ref[...] = down_wide_ref[...].astype(BF16)
 
-    gain, bias = 0.5 * wide_ref[0:1, :], 0.5 * wide_ref[1:2, :]
-
-    def body(at):
-        hat, _ = norm(x_ref[pl.ds(at, ROWS), :].astype(F32), width)
-        h = hat * gain + bias
-        act_ref[pl.ds(at, ROWS), :] = (h * half_gelu(h)[2]).astype(BF16)
-
-    chunks(block, body)
-
-
-def up_kernel(act_ref, weight_ref, narrow_ref, flags_ref, out_ref, mid_ref, z_ref, next_ref):
-    block, width = out_ref.shape
-
     def product():
-        next_ref[...] = dot(act_ref[...], weight_ref[...])
+        gain, bias = 0.5 * wide_ref[0:1, :], 0.5 * wide_ref[1:2, :]
+        for at in range(0, block, ROWS):
+            rows = slice(at, at + ROWS)
+            hat, _ = norm(x_ref[rows, :].astype(F32), width)
+            h = hat * gain + bias
+            act_ref[rows, :] = (h * half_gelu(h)[2]).astype(BF16)
+        next_ref[...] = dot(act_ref[...], up_ref[...])
 
     def keep():
         z_ref[...] = next_ref[...]
@@ -181,7 +168,7 @@
             rows = slice(at, at + ROWS)
             z = z_ref[rows, :] + shift
             out_ref[rows, :] = z
-            hat, _ = norm(z, width)
+            hat, _ = norm(z, inner)
             h = hat * gain + bias
             mid_ref[rows, :] = (h * half_gelu(h)[2] * flags_ref[rows, 0:1]).astype(BF16)
 
@@ -193,6 +180,10 @@
     padded_ref[0, 0:REACH, :] = jnp.zeros((REACH, width), BF16)
     padded_ref[0, count + REACH : count + 2 * REACH, :] = jnp.zeros((REACH, width), BF16)
     padded_ref[0, REACH : count + REACH, :] = source_ref[...]
+    fill_further(padded_ref, count)
+
+
+def fill_further(padded_ref, count):
     padded_ref[1, 0 : count + REACH, :] = padded_ref[0, DILATION : count + REACH + DILATION, :]
 
 
@@ -209,7 +200,7 @@
 def conv_kernel(*refs):
     pieces, rest_refs = refs[: len(refs) - 22], refs[len(refs) - 22 :]
     (
-        mid_ref, down_ref, cot_ref, narrow_ref, now_flags_ref, place_ref,
+        mid_hbm, down_ref, cot_ref, narrow_ref, now_flags_ref, place_ref,
         top_ref, low_ref, flat_hbm, sums_ref, wide_sums_ref,
         padded_ref, hold_ref, wide_weight_ref, weight_ref, flat_ref, taps_ref,
         out_ref, grad_ref, next_out_ref, next_grad_ref, semaphores,
@@ -222,10 +213,17 @@
 
     @pl.when(step == 0)
     def _():
+        count = mid_hbm.shape[0]
         copies = piece_copies(pieces, place_ref, hold_ref, semaphores)
+        target = padded_ref.at[0, pl.ds(REACH, count)]
+        mid_copy = pltpu.make_async_copy(mid_hbm, target, semaphores.at[devices + 1])
+        mid_copy.start()
         for copy in copies:
             copy.start()
-        fill_padded(padded_ref, mid_ref)
+        padded_ref[0, 0:REACH, :] = jnp.zeros((REACH, width), BF16)
+        padded_ref[0, count + REACH : count + 2 * REACH, :] = jnp.zeros((REACH, width), BF16)
+        mid_copy.wait()
+        fill_further(padded_ref, count)
         sums_ref[...] = jnp.zeros_like(sums_ref)
         wide_sums_ref[...] = jnp.zeros_like(wide_sums_ref)
         for copy in copies:
@@ -571,37 +569,36 @@
     conv_two = gather_stage(conv_one, axes[0])
     up_pieces = core_stage([jnp.stack(after(tuple(up_two), *conv_near))], axes)
 
-    block = 256
+    block, large = 256, 512
     steps = count // block
     wide_up = 2 * count * model * inner
     wide_conv = 2 * count * KERNEL * inner * inner
     padded = pltpu.VMEM((2, count + 2 * REACH, inner), BF16)
 
-    act_one, up_full, down_full, wide, narrow = call(
-        first_act_kernel, "first_act", steps, ("any", "any", block, "smem"),
+    act_one, up_full, down_full, wide, narrow, up_out, mid = call(
+        up_kernel, "up", steps + 1, ("any", "any", "now", "past", "smem"),
         [
-            ((count, model), BF16, block),
+            ((count, model), BF16, "now"),
             ((model, inner), BF16, None),
             ((model, inner), BF16, None),
             ((8, model), F32, None),
             ((8, inner), F32, None),
+            ((count, inner), F32, "past"),
+            ((count, inner), BF16, "past"),
         ],
         [
             pltpu.VMEM((2 * chips,) + up_block.shape, BF16),
             pltpu.VMEM((model, inner), F32),
             pltpu.VMEM((model, inner), F32),
+            pltpu.VMEM((block, inner), F32),
+            pltpu.VMEM((block, inner), F32),
             pltpu.SemaphoreType.DMA((2 * chips,)),
         ],
-        20 * count * model, (*up_pieces, inputs, after(place, conv_one)),
-    )
-    up_out, mid = call(
-        up_kernel, "up", steps + 1, ("now", None, None, "past"),
-        [((count, inner), F32, "past"), ((count, inner), BF16, "past")],
-        [pltpu.VMEM((block, inner), F32)] * 2, wide_up, (act_one, up_full, narrow, flags),
+        wide_up, (*up_pieces, inputs, flags, after(place, conv_one)),
     )
     conv_pieces = core_stage(conv_two[:1] + list(after(tuple(conv_two[1:]), mid)), axes)
     top, low, conv_flat, top_sums, cot_sums = call(
-        conv_kernel, "conv", steps + 1, ("any",) * len(conv_pieces) + (None, None, "now", None, "now", "smem"),
+        conv_kernel, "conv", steps + 1, ("any",) * len(conv_pieces) + ("any", None, "now", None, "now", "smem"),
         [
             ((count, inner), BF16, "past"),
             ((count, inner), BF16, "past"),
@@ -618,7 +615,7 @@
             pltpu.VMEM((block, KERNEL * inner), BF16),
         ]
         + [pltpu.VMEM((block, inner), F32)] * 4
-        + [pltpu.SemaphoreType.DMA((2 * chips + 1,))],
+        + [pltpu.SemaphoreType.DMA((2 * chips + 2,))],
         wide_conv + wide_up, (*conv_pieces, mid, down_full, cotangent, narrow, flags, place),
     )
     conv_kept, conv_sent = call(
@@ -635,8 +632,8 @@
         wide_conv, (low, mid, flags, place),
     )
     (output,) = call(
-        output_kernel, "output", steps, (block, block, None, None),
-        [((count, model), BF16, block)],
+        output_kernel, "output", count // large, (large, large, None, None),
+        [((count, model), BF16, large)],
         [], wide_up, (inputs, top, down_full, after(wide, conv_sent)),
     )
     conv_grad = add_up(after(conv_kept, output), [swap(conv_sent, *axes[2], 1)])

time: 228 us -> 220 us (0.965)
  local copies, waits for them, and re-layouts: 18.6 us -> 9.96 us
  Pallas kernels: 119 us -> 116 us
  waiting for transfers between devices: 23.4 us -> 26.1 us
    unnamed x52 -> x60, local copies, waits for them, and re-layouts: 14.2 us -> 5.6 us
    pallas_call x8 -> x7, Pallas kernels: 119 us -> 116 us  [call(): pl.pallas_call(kernel, name=name, grid=(grid,), in_specs=[spec(a.shape, r...]
    ppermute x38, waiting for transfers between devices: 23.4 us -> 26.1 us  [swap(): return lax.ppermute(array, axis, [(k, k ^ mask) for k in range(size)])]
  transfers between devices with their start and end apart: 38 -> 38, of which waited for: 14 -> 14; matrix products, arithmetic and copies ran while one was open for 3% -> 4% of each run, Pallas kernels for 34% -> 34%
where the time goes in v1:
time: 220 us; the launch traced here: 216 us
  Pallas kernels  116 us (53%)
  starting transfers between devices  51.8 us (24%)
  waiting for transfers between devices  26.1 us (12%)
  other arithmetic  11.2 us (5%)
  local copies, waits for them, and re-layouts  9.96 us (5%)
    pallas_call x7, Pallas kernels, call(): pl.pallas_call(kernel, name=name, grid=(grid,), in_specs=[spec(a.shape, r...  116 us
    ppermute x38, starting transfers between devices, swap(): return lax.ppermute(array, axis, [(k, k ^ mask) for k in range(size)])  51.8 us
    ppermute x38, waiting for transfers between devices, swap(): return lax.ppermute(array, axis, [(k, k ^ mask) for k in range(size)])  26.1 us
    another operation x5, other arithmetic  5.71 us
    unnamed x60, local copies, waits for them, and re-layouts  5.6 us
  transfers between devices with their start and end apart: 38, of which 14 were waited for; matrix products, arithmetic and copies ran while one was open for 4% of the time, Pallas kernels for 34%

profile of v1, /device:TPU:0, one launch (start us, length us, event | category | flops | bytes accessed | tf_op | source)
XLA Modules:
  0.0 216.4 jit_solution(8477379861072335171)
XLA Ops:
  0.6 0.9 fusion.22
  1.6 4.1 %collective-permute-start.2 = (bf16[88,640]{1,0:T(8,128)(2,1)S(1)}, bf16[88,640]{1,0:T(8,128)(2,1)S(1)}, u32[]{:S(2)}, u32[]{:S(2)}) collective-permute-start(bf16[88,640]{1,0:T(8,128)(2,1)S(1)} %fusion.22), channel_id=1, source_target_pairs={{0,4},{2,6},{4,0},{6,2},{1,5},{3,7},{5,1},{7,3},{8,12},{10,14},{12... | collective-permute-start | bytes 337928 | tf_op jit(solution)/shard_map/ppermute | solution.py:24
  5.7 1.6 collective-permute-start.1
  7.3 1.0 fusion.32
  8.2 4.6 %collective-permute-done.2 = bf16[88,640]{1,0:T(8,128)(2,1)S(1)} collective-permute-done((bf16[88,640]{1,0:T(8,128)(2,1)S(1)}, bf16[88,640]{1,0:T(8,128)(2,1)S(1)}, u32[]{:S(2)}, u32[]{:S(2)}) %collective-permute-start.2) | collective-permute-done | bytes 112672 | tf_op jit(solution)/shard_map/ppermute | solution.py:24
  12.8 1.9 collective-permute-done.3
  14.9 2.5 %collective-permute-start.8 = (bf16[4,88,640]{2,1,0:T(8,128)(2,1)S(1)}, bf16[4,88,640]{2,1,0:T(8,128)(2,1)S(1)}, u32[]{:S(2)}, u32[]{:S(2)}) collective-permute-start(bf16[4,88,640]{2,1,0:T(8,128)(2,1)S(1)} %pad_maximum_fusion.2), channel_id=1, source_target_pairs={{0,24},{8,16},{16,8},{24,0},{1,25},{9,17},{17,9},{25,1},{2,26},{10... | collective-permute-start | bytes 1351688 | tf_op jit(solution)/shard_map/ppermute | solution.py:24
  17.4 0.5 collective-permute-start.7
  17.9 0.5 collective-permute-start.6
  18.4 0.9 reshape.253
  19.4 2.0 collective-permute-start
  21.4 3.4 %collective-permute-start.5 = (bf16[104,640]{1,0:T(8,128)(2,1)S(1)}, bf16[104,640]{1,0:T(8,128)(2,1)S(1)}, u32[]{:S(2)}, u32[]{:S(2)}) collective-permute-start(bf16[104,640]{1,0:T(8,128)(2,1)S(1)} %pad.44), channel_id=1, source_target_pairs={{0,6},{2,4},{4,2},{6,0},{1,7},{3,5},{5,3},{7,1},{8,14},{10,12},{12... | collective-permute-start | bytes 399368 | tf_op jit(solution)/shard_map/ppermute | solution.py:24
  24.8 5.0 %collective-permute-start.4 = (bf16[104,640]{1,0:T(8,128)(2,1)S(1)}, bf16[104,640]{1,0:T(8,128)(2,1)S(1)}, u32[]{:S(2)}, u32[]{:S(2)}) collective-permute-start(bf16[104,640]{1,0:T(8,128)(2,1)S(1)} %pad.44), channel_id=1, source_target_pairs={{0,4},{2,6},{4,0},{6,2},{1,5},{3,7},{5,1},{7,3},{8,12},{10,14},{12... | collective-permute-start | bytes 399368 | tf_op jit(solution)/shard_map/ppermute | solution.py:24
  29.8 0.8 reduce-window.8
  30.8 0.9 collective-permute-done.5
  31.7 3.4 %collective-permute-done.4 = bf16[104,640]{1,0:T(8,128)(2,1)S(1)} collective-permute-done((bf16[104,640]{1,0:T(8,128)(2,1)S(1)}, bf16[104,640]{1,0:T(8,128)(2,1)S(1)}, u32[]{:S(2)}, u32[]{:S(2)}) %collective-permute-start.4) | collective-permute-done | bytes 133152 | tf_op jit(solution)/shard_map/ppermute | solution.py:24
  35.1 1.6 collective-permute-done.7
  36.9 1.3 pad_maximum_fusion.own_pieces
  38.6 1.6 collective-permute-start.11
  40.2 1.4 collective-permute-start.10
  41.6 0.5 collective-permute-start.9
  42.3 0.4 copy.38
  42.7 1.1 concatenate.10.flags_ref.refs_12_.now_flags_ref
  43.8 0.6 pad_add_fusion.place_ref.refs_13_
  44.4 18.7 %up.1 = (bf16[2048,1280]{1,0:T(8,128)(2,1)}, bf16[1280,640]{1,0:T(8,128)(2,1)}, bf16[1280,640]{1,0:T(8,128)(2,1)}, f32[8,1280]{1,0:T(8,128)}, f32[8,640]{1,0:T(8...) custom-call(bf16[4,4,88,640]{3,2,1,0:T(8,128)(2,1)} %copy-done.13, ...), custom_call_target="tpu_custom_call" | custom-call | flops 3355443200 | bytes 25358348 | tf_op jit(solution)/shard_map/up/pallas_call | solution.py:483
  63.1 2.4 %collective-permute-done.10.refs_2_ = bf16[4,104,640]{2,1,0:T(8,128)(2,1)} collective-permute-done((bf16[4,104,640]{2,1,0:T(8,128)(2,1)S(1)}, bf16[4,104,640]{2,1,0:T(8,128)(2,1)}, u32[]{:S(2)}, u32[]{:S(2)}) %collective-permute-start.10) | collective-permute-done | bytes 532512 | tf_op jit(solution)/shard_map/ppermute | solution.py:24
  65.6 0.5 collective-permute-start.15
  66.1 1.6 collective-permute-done.14.refs_5_
  67.7 1.5 collective-permute-done.15.refs_6_
  69.2 0.8 copy-done.22
  70.2 29.0 %conv.1 = (bf16[2048,640]{1,0:T(8,128)(2,1)}, bf16[2048,640]{1,0:T(8,128)(2,1)}, bf16[640,3200]{1,0:T(8,128)(2,1)}, f32[24,640]{1,0:T(8,128)}, f32[8,1280]{1,0:T(8,128)}) custom-call(bf16[4,104,640]{2,1,0:T(8,128)(2,1)} %copy-done.14, bf16[4,104,640]{2,1,0:T(8,128)(2,1)} %collective-permute-done.9.refs_1_, ...), custom_call_target="tpu_custom_call" | custom-call | flops 11744051200 | bytes 23289868 | tf_op jit(solution)/shard_map/conv/pallas_call | solution.py:483
  99.2 1.9 copy-done.11
  101.1 12.9 %weights.1 = (bf16[4,4,104,640]{3,2,1,0:T(8,128)(2,1)S(1)}, bf16[4,4,104,640]{3,2,1,0:T(8,128)(2,1)S(1)}) custom-call(bf16[2048,640]{1,0:T(8,128)(2,1)S(1)} %copy-done.11, bf16[2048,640]{1,0:T(8,128)(2,1)} %get-tuple-element.73.refs_8_.mid_ref, f32[2048,8]{1,0:T(8,128)S(1)} %copy-done.4, s32[3]{0:T(128)S(1)} %copy-done.8), custom_call_target="tpu_custom_call" | custom-call | flops 8388608000 | bytes 9568268 | tf_op jit(solution)/shard_map/weights/pallas_call | solution.py:483
  114.2 6.0 %output.1 = bf16[2048,1280]{1,0:T(8,128)(2,1)} custom-call(bf16[2048,1280]{1,0:T(8,128)(2,1)S(1)} %bitcast.125, bf16[2048,640]{1,0:T(8,128)(2,1)S(1)} %copy-done, bf16[1280,640]{1,0:T(8,128)(2,1)S(1)} %copy-done.2, f32[8,1280]{1,0:T(8,128)S(1)} %copy-done.5), custom_call_target="tpu_custom_call" | custom-call | flops 3355443200 | bytes 14786560 | tf_op jit(solution)/shard_map/output/pallas_call | solution.py:483
  120.2 2.8 %fusion.26 = (bf16[4,4,104,640]{3,2,1,0:T(8,128)(2,1)S(1)}, f32[4,4,104,640]{3,2,1,0:T(8,128)}) fusion(bf16[4,4,104,640]{3,2,1,0:T(8,128)(2,1)S(1)} %collective-permute-done.17, bf16[4,4,104,640]{3,2,1,0:T(8,128)(2,1)S(1)} %get-tuple-element.87), kind=kLoop, calls=%fused_computation.85 | loop fusion | flops 4259840 | bytes 10649600 | tf_op jit(solution)/shard_map/convert.13
  123.1 1.7 collective-permute-start.20
  124.8 1.4 collective-permute-start.19
  126.2 0.5 collective-permute-start.18
  126.7 2.6 %copy-done.9 = f32[2048,640]{1,0:T(8,128)S(1)} copy-done((f32[2048,640]{1,0:T(8,128)S(1)}, f32[2048,640]{1,0:T(8,128)}, u32[]{:S(2)}) %copy-start.9) | copy-done | bytes 5242904
  129.4 17.6 %mid_grad.1 = (bf16[2048,640]{1,0:T(8,128)(2,1)S(1)}, f32[24,640]{1,0:T(8,128)S(1)}) custom-call(bf16[2048,640]{1,0:T(8,128)(2,1)S(1)} %copy-done.11, bf16[640,3200]{1,0:T(8,128)(2,1)S(1)} %copy-done.10, f32[2048,640]{1,0:T(8,128)S(1)} %copy-done.9, f32[8,640]{1,0:T(8,128)S(1)} %copy-done.12, f32[2048,8]{1,0:T(8,128)S(1)} %copy-done.4, f32[2048,8]{1,0:T(8,128)S(1)} %copy-done.4), custom_call_target="tpu_custom_call" | custom-call | flops 8388608000 | bytes 14794752 | tf_op jit(solution)/shard_map/mid_grad/pallas_call | solution.py:483
  147.1 10.8 %up_weight.1 = (bf16[4,4,2,40,640]{4,3,2,1,0:T(8,128)(2,1)S(1)}, bf16[4,4,2,40,640]{4,3,2,1,0:T(8,128)(2,1)S(1)}) custom-call(bf16[2048,1280]{1,0:T(8,128)(2,1)S(1)} %bitcast.129, bf16[2048,1280]{1,0:T(8,128)(2,1)S(1)} %bitcast.127, bf16[2048,640]{1,0:T(8,128)(2,1)S(1)} %get-tuple-element.89.low_ref.up_low_ref, bf16[2048,640]{1,0:T(8,128)(2,1)S(1)} %copy-done.1, ...), custom_call_target="tpu_custom_call" | custom-call | flops 1 | bytes 1 | tf_op jit(solution)/shard_map/up_weight/pallas_call | solution.py:483
  158.0 1.5 fusion.29
  159.6 2.5 %collective-permute-start.27 = (bf16[104,640]{1,0:T(8,128)(2,1)S(1)}, bf16[104,640]{1,0:T(8,128)(2,1)S(1)}, u32[]{:S(2)}, u32[]{:S(2)}) collective-permute-start(bf16[104,640]{1,0:T(8,128)(2,1)S(1)} %get-tuple-element.131), channel_id=1, source_target_pairs={{0,6},{2,4},{4,2},{6,0},{1,7},{3,5},{5,3},{7,1},{8,14},{10,12},{12... | collective-permute-start | bytes 399368 | tf_op jit(solution)/shard_map/ppermute | solution.py:24
  162.1 2.6 %collective-permute-start.26 = (bf16[104,640]{1,0:T(8,128)(2,1)S(1)}, bf16[104,640]{1,0:T(8,128)(2,1)S(1)}, u32[]{:S(2)}, u32[]{:S(2)}) collective-permute-start(bf16[104,640]{1,0:T(8,128)(2,1)S(1)} %get-tuple-element.132), channel_id=1, source_target_pairs={{0,4},{2,6},{4,0},{6,2},{1,5},{3,7},{5,1},{7,3},{8,12},{10,14},{12... | collective-permute-start | bytes 399368 | tf_op jit(solution)/shard_map/ppermute | solution.py:24
  165.3 1.6 collective-permute-start.24
  166.9 1.4 collective-permute-start.23
  168.3 0.5 collective-permute-start.22
  168.9 4.8 %collective-permute-start.25 = (bf16[104,640]{1,0:T(8,128)(2,1)S(1)}, bf16[104,640]{1,0:T(8,128)(2,1)S(1)}, u32[]{:S(2)}, u32[]{:S(2)}) collective-permute-start(bf16[104,640]{1,0:T(8,128)(2,1)S(1)} %get-tuple-element.133), channel_id=1, source_target_pairs={{0,2},{2,0},{4,6},{6,4},{1,3},{3,1},{5,7},{7,5},{8,10},{10,8},{12,... | collective-permute-start | bytes 399368 | tf_op jit(solution)/shard_map/ppermute | solution.py:24
  173.7 20.7 %input_grad.1 = (f32[2048,1280]{1,0:T(8,128)}, f32[4,4,16,128]{3,2,1,0:T(8,128)S(1)}, f32[4,4,16,128]{3,2,1,0:T(8,128)S(1)}) custom-call(bf16[2048,640]{1,0:T(8,128)(2,1)S(1)} %get-tuple-element.89.low_ref.up_low_ref, bf16[1280,640]{1,0:T(8,128)(2,1)S(1)} %copy-done.3, bf16[2048,1280]{1,0:T(8,128)(2,1)S(1)} %bitcast.125, bf16[2048,1280]{1,0:T(8,128)(2,1)S(1)} %bitcast.127, ...), custom_call_target="tpu_custom_call" | custom-call | flops 3355443200 | bytes 25698316 | tf_op jit(solution)/shard_map/input_grad/pallas_call | solution.py:483
  194.7 0.7 reshape.256
  195.7 2.5 %collective-permute-start.30 = (bf16[2,40,640]{2,1,0:T(8,128)(2,1)S(1)}, bf16[2,40,640]{2,1,0:T(8,128)(2,1)S(1)}, u32[]{:S(2)}, u32[]{:S(2)}) collective-permute-start(bf16[2,40,640]{2,1,0:T(8,128)(2,1)S(1)} %get-tuple-element.135), channel_id=1, source_target_pairs={{0,6},{2,4},{4,2},{6,0},{1,7},{3,5},{5,3},{7,1},{8,14},{10,12},{12... | collective-permute-start | bytes 307208 | tf_op jit(solution)/shard_map/ppermute | solution.py:24
  198.1 0.9 collective-permute-start.29
  199.1 1.4 collective-permute-start.33
  200.5 1.6 collective-permute-start.34
  202.1 0.5 collective-permute-start.32
  202.7 1.5 collective-permute-done.30
  204.1 4.5 %collective-permute-done.29 = bf16[2,40,640]{2,1,0:T(8,128)(2,1)S(1)} collective-permute-done((bf16[2,40,640]{2,1,0:T(8,128)(2,1)S(1)}, bf16[2,40,640]{2,1,0:T(8,128)(2,1)S(1)}, u32[]{:S(2)}, u32[]{:S(2)}) %collective-permute-start.29) | collective-permute-done | bytes 102432 | tf_op jit(solution)/shard_map/ppermute | solution.py:24
  208.9 2.5 %collective-permute-start.37 = (f32[16,128]{1,0:T(8,128)S(1)}, f32[16,128]{1,0:T(8,128)S(1)}, u32[]{:S(2)}, u32[]{:S(2)}) collective-permute-start(f32[16,128]{1,0:T(8,128)S(1)} %get-tuple-element.143), channel_id=1, source_target_pairs={{0,6},{2,4},{4,2},{6,0},{1,7},{3,5},{5,3},{7,1},{8,14},{10,12},{12... | collective-permute-start | bytes 24584 | tf_op jit(solution)/shard_map/ppermute | solution.py:24
  211.4 0.9 collective-permute-start.35
  212.3 0.7 slice_bitcast_fusion.13
  213.4 1.0 collective-permute-done.37
  214.4 0.6 collective-permute-done.35
  215.0 0.5 slice_bitcast_fusion.26
  215.6 0.5 slice_bitcast_fusion.27
  (125 shorter events, 3.4 us)
Async XLA Ops:
  1.6 11.3 %collective-permute-start.2 = (bf16[88,640]{1,0:T(8,128)(2,1)S(1)}, bf16[88,640]{1,0:T(8,128)(2,1)S(1)}, u32[]{:S(2)}, u32[]{:S(2)}) collective-permute-start(bf16[88,640]{1,0:T(8,128)(2,1)S(1)} %fusion.22), channel_id=1, source_target_pairs={{0,4},{2,6},{4,0},{6,2},{1,5},{3,7},{5,1},{7,3},{8,12},{10,14},{12... | collective-permute-start | bytes 337928 | tf_op jit(solution)/shard_map/ppermute | solution.py:24
  5.7 7.2 %collective-permute-start.1 = (bf16[88,640]{1,0:T(8,128)(2,1)S(1)}, bf16[88,640]{1,0:T(8,128)(2,1)S(1)}, u32[]{:S(2)}, u32[]{:S(2)}) collective-permute-start(bf16[88,640]{1,0:T(8,128)(2,1)S(1)} %fusion.22), channel_id=1, source_target_pairs={{0,2},{2,0},{4,6},{6,4},{1,3},{3,1},{5,7},{7,5},{8,10},{10,8},{12,... | collective-permute-start | bytes 337928 | tf_op jit(solution)/shard_map/ppermute | solution.py:24
  7.3 7.5 %collective-permute-start.3 = (bf16[88,640]{1,0:T(8,128)(2,1)S(1)}, bf16[88,640]{1,0:T(8,128)(2,1)S(1)}, u32[]{:S(2)}, u32[]{:S(2)}) collective-permute-start(bf16[88,640]{1,0:T(8,128)(2,1)S(1)} %fusion.22), channel_id=1, source_target_pairs={{0,6},{2,4},{4,2},{6,0},{1,7},{3,5},{5,3},{7,1},{8,14},{10,12},{12... | collective-permute-start | bytes 337928 | tf_op jit(solution)/shard_map/ppermute | solution.py:24
  14.8 23.6 %copy-start.19 = (s32[2048]{0:T(1024)S(1)}, s32[2048]{0:T(1024)}, u32[]{:S(2)}) copy-start(s32[2048]{0:T(1024)} %param.18) | copy-start | bytes 24580
  14.9 20.2 %collective-permute-start.8 = (bf16[4,88,640]{2,1,0:T(8,128)(2,1)S(1)}, bf16[4,88,640]{2,1,0:T(8,128)(2,1)S(1)}, u32[]{:S(2)}, u32[]{:S(2)}) collective-permute-start(bf16[4,88,640]{2,1,0:T(8,128)(2,1)S(1)} %pad_maximum_fusion.2), channel_id=1, source_target_pairs={{0,24},{8,16},{16,8},{24,0},{1,25},{9,17},{17,9},{25,1},{2,26},{10... | collective-permute-start | bytes 1351688 | tf_op jit(solution)/shard_map/ppermute | solution.py:24
  17.4 19.3 %collective-permute-start.7 = (bf16[4,88,640]{2,1,0:T(8,128)(2,1)S(1)}, bf16[4,88,640]{2,1,0:T(8,128)(2,1)S(1)}, u32[]{:S(2)}, u32[]{:S(2)}) collective-permute-start(bf16[4,88,640]{2,1,0:T(8,128)(2,1)S(1)} %pad_maximum_fusion.2), channel_id=1, source_target_pairs={{0,16},{8,24},{16,0},{24,8},{1,17},{9,25},{17,1},{25,9},{2,18},{10... | collective-permute-start | bytes 1351688 | tf_op jit(solution)/shard_map/ppermute | solution.py:24
  17.9 19.0 %collective-permute-start.6 = (bf16[4,88,640]{2,1,0:T(8,128)(2,1)S(1)}, bf16[4,88,640]{2,1,0:T(8,128)(2,1)}, u32[]{:S(2)}, u32[]{:S(2)}) collective-permute-start(bf16[4,88,640]{2,1,0:T(8,128)(2,1)S(1)} %pad_maximum_fusion.2), channel_id=1, source_target_pairs={{0,8},{8,0},{16,24},{24,16},{1,9},{9,1},{17,25},{25,17},{2,10},{10... | collective-permute-start | bytes 1351688 | tf_op jit(solution)/shard_map/ppermute | solution.py:24
  19.4 5.4 %collective-permute-start = (bf16[104,640]{1,0:T(8,128)(2,1)S(1)}, bf16[104,640]{1,0:T(8,128)(2,1)S(1)}, u32[]{:S(2)}, u32[]{:S(2)}) collective-permute-start(bf16[104,640]{1,0:T(8,128)(2,1)S(1)} %pad.44), channel_id=1, source_target_pairs={{0,2},{2,0},{4,6},{6,4},{1,3},{3,1},{5,7},{7,5},{8,10},{10,8},{12,... | collective-permute-start | bytes 399368 | tf_op jit(solution)/shard_map/ppermute | solution.py:24
  21.4 10.3 %collective-permute-start.5 = (bf16[104,640]{1,0:T(8,128)(2,1)S(1)}, bf16[104,640]{1,0:T(8,128)(2,1)S(1)}, u32[]{:S(2)}, u32[]{:S(2)}) collective-permute-start(bf16[104,640]{1,0:T(8,128)(2,1)S(1)} %pad.44), channel_id=1, source_target_pairs={{0,6},{2,4},{4,2},{6,0},{1,7},{3,5},{5,3},{7,1},{8,14},{10,12},{12... | collective-permute-start | bytes 399368 | tf_op jit(solution)/shard_map/ppermute | solution.py:24
  24.8 10.3 %collective-permute-start.4 = (bf16[104,640]{1,0:T(8,128)(2,1)S(1)}, bf16[104,640]{1,0:T(8,128)(2,1)S(1)}, u32[]{:S(2)}, u32[]{:S(2)}) collective-permute-start(bf16[104,640]{1,0:T(8,128)(2,1)S(1)} %pad.44), channel_id=1, source_target_pairs={{0,4},{2,6},{4,0},{6,2},{1,5},{3,7},{5,1},{7,3},{8,12},{10,14},{12... | collective-permute-start | bytes 399368 | tf_op jit(solution)/shard_map/ppermute | solution.py:24
  31.7 5.2 %copy-start.15 = (bf16[104,640]{1,0:T(8,128)(2,1)}, bf16[104,640]{1,0:T(8,128)(2,1)S(1)}, u32[]{:S(2)}) copy-start(bf16[104,640]{1,0:T(8,128)(2,1)S(1)} %collective-permute-done.5) | copy-start | bytes 399364
  35.1 1.8 copy-start.17
  38.2 6.2 %copy-start.13 = (bf16[4,4,88,640]{3,2,1,0:T(8,128)(2,1)}, bf16[4,4,88,640]{3,2,1,0:T(8,128)(2,1)S(1)}, u32[]{:S(2)}) copy-start(bf16[4,4,88,640]{3,2,1,0:T(8,128)(2,1)S(1)} %pad_maximum_fusion.own_pieces) | copy-start | bytes 5406724
  38.2 6.1 %collective-permute-start.12 = (bf16[4,4,88,640]{3,2,1,0:T(8,128)(2,1)S(1)}, bf16[4,4,88,640]{3,2,1,0:T(8,128)(2,1)}, u32[]{:S(2)}, u32[]{:S(2)}) collective-permute-start(bf16[4,4,88,640]{3,2,1,0:T(8,128)(2,1)S(1)} %pad_maximum_fusion.own_pieces), channel_id=1, source_target_pairs={{0,1},{1,0},{2,3},{3,2},{4,5},{5,4},{6,7},{7,6},{8,9},{9,8},{10,11... | collective-permute-start | bytes 5406728 | tf_op jit(solution)/shard_map/ppermute | solution.py:24
  38.6 24.6 %copy-start.14 = (bf16[4,104,640]{2,1,0:T(8,128)(2,1)}, bf16[4,104,640]{2,1,0:T(8,128)(2,1)S(1)}, u32[]{:S(2)}) copy-start(bf16[4,104,640]{2,1,0:T(8,128)(2,1)S(1)} %pad_maximum_fusion.1.refs_0_) | copy-start | bytes 1597444
  38.6 24.6 %collective-permute-start.11 = (bf16[4,104,640]{2,1,0:T(8,128)(2,1)S(1)}, bf16[4,104,640]{2,1,0:T(8,128)(2,1)S(1)}, u32[]{:S(2)}, u32[]{:S(2)}) collective-permute-start(bf16[4,104,640]{2,1,0:T(8,128)(2,1)S(1)} %pad_maximum_fusion.1.refs_0_), channel_id=1, source_target_pairs={{0,24},{8,16},{16,8},{24,0},{1,25},{9,17},{17,9},{25,1},{2,26},{10... | collective-permute-start | bytes 1597448 | tf_op jit(solution)/shard_map/ppermute | solution.py:24
  40.2 25.3 %collective-permute-start.10 = (bf16[4,104,640]{2,1,0:T(8,128)(2,1)S(1)}, bf16[4,104,640]{2,1,0:T(8,128)(2,1)}, u32[]{:S(2)}, u32[]{:S(2)}) collective-permute-start(bf16[4,104,640]{2,1,0:T(8,128)(2,1)S(1)} %pad_maximum_fusion.1.refs_0_), channel_id=1, source_target_pairs={{0,16},{8,24},{16,0},{24,8},{1,17},{9,25},{17,1},{25,9},{2,18},{10... | collective-permute-start | bytes 1597448 | tf_op jit(solution)/shard_map/ppermute | solution.py:24
  41.6 23.9 %collective-permute-start.9 = (bf16[4,104,640]{2,1,0:T(8,128)(2,1)S(1)}, bf16[4,104,640]{2,1,0:T(8,128)(2,1)}, u32[]{:S(2)}, u32[]{:S(2)}) collective-permute-start(bf16[4,104,640]{2,1,0:T(8,128)(2,1)S(1)} %pad_maximum_fusion.1.refs_0_), channel_id=1, source_target_pairs={{0,8},{8,0},{16,24},{24,16},{1,9},{9,1},{17,25},{25,17},{2,10},{10... | collective-permute-start | bytes 1597448 | tf_op jit(solution)/shard_map/ppermute | solution.py:24
  44.4 21.7 %collective-permute-start.13 = (bf16[4,104,640]{2,1,0:T(8,128)(2,1)S(1)}, bf16[4,104,640]{2,1,0:T(8,128)(2,1)}, u32[]{:S(2)}, u32[]{:S(2)}) collective-permute-start(bf16[4,104,640]{2,1,0:T(8,128)(2,1)S(1)} %pad_maximum_fusion.1.refs_0_), channel_id=1, source_target_pairs={{0,1},{1,0},{2,3},{3,2},{4,5},{5,4},{6,7},{7,6},{8,9},{9,8},{10,11... | collective-permute-start | bytes 1597448 | tf_op jit(solution)/shard_map/ppermute | solution.py:24
  63.1 7.0 %copy-start.20 = (bf16[4,104,640]{2,1,0:T(8,128)(2,1)}, bf16[4,104,640]{2,1,0:T(8,128)(2,1)S(1)}, u32[]{:S(2)}) copy-start(bf16[4,104,640]{2,1,0:T(8,128)(2,1)S(1)} %collective-permute-done.11.refs_3_) | copy-start | bytes 1597444
  65.5 2.1 collective-permute-start.14
  65.6 3.6 %collective-permute-start.15 = (bf16[4,104,640]{2,1,0:T(8,128)(2,1)}, bf16[4,104,640]{2,1,0:T(8,128)(2,1)S(1)}, u32[]{:S(2)}, u32[]{:S(2)}) collective-permute-start(bf16[4,104,640]{2,1,0:T(8,128)(2,1)} %collective-permute-done.10.refs_2_), channel_id=1, source_target_pairs={{0,1},{1,0},{2,3},{3,2},{4,5},{5,4},{6,7},{7,6},{8,9},{9,8},{10,11... | collective-permute-start | bytes 1597448 | tf_op jit(solution)/shard_map/ppermute | solution.py:24
  66.0 3.1 %collective-permute-start.16 = (bf16[4,104,640]{2,1,0:T(8,128)(2,1)S(1)}, bf16[4,104,640]{2,1,0:T(8,128)(2,1)S(1)}, u32[]{:S(2)}, u32[]{:S(2)}) collective-permute-start(bf16[4,104,640]{2,1,0:T(8,128)(2,1)S(1)} %collective-permute-done.11.refs_3_), channel_id=1, source_target_pairs={{0,1},{1,0},{2,3},{3,2},{4,5},{5,4},{6,7},{7,6},{8,9},{9,8},{10,11... | collective-permute-start | bytes 1597448 | tf_op jit(solution)/shard_map/ppermute | solution.py:24
  67.7 2.5 %copy-start.21 = (bf16[4,104,640]{2,1,0:T(8,128)(2,1)}, bf16[4,104,640]{2,1,0:T(8,128)(2,1)S(1)}, u32[]{:S(2)}) copy-start(bf16[4,104,640]{2,1,0:T(8,128)(2,1)S(1)} %collective-permute-done.14.refs_5_) | copy-start | bytes 1597444
  70.2 29.0 %copy-start.4 = (f32[2048,8]{1,0:T(8,128)S(1)}, f32[2048,8]{1,0:T(8,128)}, u32[]{:S(2)}) copy-start(f32[2048,8]{1,0:T(8,128)} %concatenate.10.flags_ref.refs_12_.now_flags_ref) | copy-start | bytes 196612
  70.2 29.0 %copy-start.8 = (s32[3]{0:T(128)S(1)}, s32[3]{0:T(128)}, u32[]{:S(2)}) copy-start(s32[3]{0:T(128)} %pad_add_fusion.place_ref.refs_13_) | copy-start | bytes 40
  99.1 15.1 %slice-start = ((s8[5242880]{0:T(1024)(128)(4,1)}), s8[4194304]{0:T(1024)(128)(4,1)S(1)}, s32[]{:S(2)}) async-start(s8[5242880]{0:T(1024)(128)(4,1)} %bitcast.124), calls=%async_computation | async-start | bytes 8388608
  99.2 1.9 copy-start.11
  101.1 13.1 %slice-start.1 = ((s8[5242880]{0:T(1024)(128)(4,1)}), s8[1048576]{0:T(1024)(128)(4,1)S(1)}, s32[]{:S(2)}) async-start(s8[5242880]{0:T(1024)(128)(4,1)} %bitcast.124), calls=%async_computation.1 | async-start | bytes 2097152
  101.1 13.1 %copy-start = (bf16[2048,640]{1,0:T(8,128)(2,1)S(1)}, bf16[2048,640]{1,0:T(8,128)(2,1)}, u32[]{:S(2)}) copy-start(bf16[2048,640]{1,0:T(8,128)(2,1)} %get-tuple-element.79.top_ref) | copy-start | bytes 7864324
  101.1 13.1 %copy-start.2 = (bf16[1280,640]{1,0:T(8,128)(2,1)S(1)}, bf16[1280,640]{1,0:T(8,128)(2,1)}, u32[]{:S(2)}) copy-start(bf16[1280,640]{1,0:T(8,128)(2,1)} %get-tuple-element.77.refs_9_.weight_ref) | copy-start | bytes 4915204
  101.1 13.2 %copy-start.5 = (f32[8,1280]{1,0:T(8,128)S(1)}, f32[8,1280]{1,0:T(8,128)}, u32[]{:S(2)}) copy-start(f32[8,1280]{1,0:T(8,128)} %get-tuple-element.83.wide_ref) | copy-start | bytes 122884
  114.0 6.2 %collective-permute-start.17 = (bf16[4,4,104,640]{3,2,1,0:T(8,128)(2,1)S(1)}, bf16[4,4,104,640]{3,2,1,0:T(8,128)(2,1)S(1)}, u32[]{:S(2)}, u32[]{:S(2)}) collective-permute-start(bf16[4,4,104,640]{3,2,1,0:T(8,128)(2,1)S(1)} %get-tuple-element.82), channel_id=1, source_target_pairs={{0,1},{1,0},{2,3},{3,2},{4,5},{5,4},{6,7},{7,6},{8,9},{9,8},{10,11... | collective-permute-start | bytes 6389768 | tf_op jit(solution)/shard_map/ppermute | solution.py:24
  120.2 6.5 %copy-start.10 = (bf16[640,3200]{1,0:T(8,128)(2,1)S(1)}, bf16[640,3200]{1,0:T(8,128)(2,1)}, u32[]{:S(2)}) copy-start(bf16[640,3200]{1,0:T(8,128)(2,1)} %get-tuple-element.84.flat_ref) | copy-start | bytes 12288004
  123.0 3.7 %copy-start.12 = (f32[8,640]{1,0:T(8,128)S(1)}, f32[8,640]{1,0:T(8,128)}, u32[]{:S(2)}) copy-start(f32[8,640]{1,0:T(8,128)} %get-tuple-element.88.refs_11_.narrow_ref) | copy-start | bytes 61444
  123.1 34.8 %collective-permute-start.20 = (bf16[4,104,640]{2,1,0:T(8,128)(2,1)S(1)}, bf16[4,104,640]{2,1,0:T(8,128)(2,1)S(1)}, u32[]{:S(2)}, u32[]{:S(2)}) collective-permute-start(bf16[4,104,640]{2,1,0:T(8,128)(2,1)S(1)} %get-tuple-element.125), channel_id=1, source_target_pairs={{0,24},{8,16},{16,8},{24,0},{1,25},{9,17},{17,9},{25,1},{2,26},{10... | collective-permute-start | bytes 1597448 | tf_op jit(solution)/shard_map/ppermute | solution.py:24
  124.8 33.1 %collective-permute-start.19 = (bf16[4,104,640]{2,1,0:T(8,128)(2,1)S(1)}, bf16[4,104,640]{2,1,0:T(8,128)(2,1)S(1)}, u32[]{:S(2)}, u32[]{:S(2)}) collective-permute-start(bf16[4,104,640]{2,1,0:T(8,128)(2,1)S(1)} %get-tuple-element.126), channel_id=1, source_target_pairs={{0,16},{8,24},{16,0},{24,8},{1,17},{9,25},{17,1},{25,9},{2,18},{10... | collective-permute-start | bytes 1597448 | tf_op jit(solution)/shard_map/ppermute | solution.py:24
  126.2 31.7 %collective-permute-start.18 = (bf16[4,104,640]{2,1,0:T(8,128)(2,1)S(1)}, bf16[4,104,640]{2,1,0:T(8,128)(2,1)S(1)}, u32[]{:S(2)}, u32[]{:S(2)}) collective-permute-start(bf16[4,104,640]{2,1,0:T(8,128)(2,1)S(1)} %get-tuple-element.127), channel_id=1, source_target_pairs={{0,8},{8,0},{16,24},{24,16},{1,9},{9,1},{17,25},{25,17},{2,10},{10... | collective-permute-start | bytes 1597448 | tf_op jit(solution)/shard_map/ppermute | solution.py:24
  126.7 20.3 %slice-start.2 = ((s8[5242880]{0:T(1024)(128)(4,1)}), s8[4194304]{0:T(1024)(128)(4,1)S(1)}, s32[]{:S(2)}) async-start(s8[5242880]{0:T(1024)(128)(4,1)} %bitcast.126), calls=%async_computation.2 | async-start | bytes 8388608
  126.7 20.3 %slice-start.4 = ((s8[5242880]{0:T(1024)(128)(4,1)}), s8[4194304]{0:T(1024)(128)(4,1)S(1)}, s32[]{:S(2)}) async-start(s8[5242880]{0:T(1024)(128)(4,1)} %bitcast.128), calls=%async_computation.4 | async-start | bytes 8388608
  126.7 2.6 %copy-start.9 = (f32[2048,640]{1,0:T(8,128)S(1)}, f32[2048,640]{1,0:T(8,128)}, u32[]{:S(2)}) copy-start(f32[2048,640]{1,0:T(8,128)} %get-tuple-element.85.up_out_ref) | copy-start | bytes 15728644
  129.4 17.7 %slice-start.3 = ((s8[5242880]{0:T(1024)(128)(4,1)}), s8[1048576]{0:T(1024)(128)(4,1)S(1)}, s32[]{:S(2)}) async-start(s8[5242880]{0:T(1024)(128)(4,1)} %bitcast.126), calls=%async_computation.3 | async-start | bytes 2097152
  129.4 17.7 %copy-start.1 = (bf16[2048,640]{1,0:T(8,128)(2,1)S(1)}, bf16[2048,640]{1,0:T(8,128)(2,1)}, u32[]{:S(2)}) copy-start(bf16[2048,640]{1,0:T(8,128)(2,1)} %get-tuple-element.79.top_ref) | copy-start | bytes 7864324
  129.4 17.7 %slice-start.5 = ((s8[5242880]{0:T(1024)(128)(4,1)}), s8[1048576]{0:T(1024)(128)(4,1)S(1)}, s32[]{:S(2)}) async-start(s8[5242880]{0:T(1024)(128)(4,1)} %bitcast.128), calls=%async_computation.5 | async-start | bytes 2097152
  157.9 6.8 %collective-permute-start.21 = (bf16[4,4,2,40,640]{4,3,2,1,0:T(8,128)(2,1)S(1)}, bf16[4,4,2,40,640]{4,3,2,1,0:T(8,128)(2,1)S(1)}, u32[]{:S(2)}, u32[]{:S(2)}) collective-permute-start(bf16[4,4,2,40,640]{4,3,2,1,0:T(8,128)(2,1)S(1)} %get-tuple-element.100), channel_id=1, source_target_pairs={{0,1},{1,0},{2,3},{3,2},{4,5},{5,4},{6,7},{7,6},{8,9},{9,8},{10,11... | collective-permute-start | bytes 4915208 | tf_op jit(solution)/shard_map/ppermute | solution.py:24
  159.6 9.3 %collective-permute-start.27 = (bf16[104,640]{1,0:T(8,128)(2,1)S(1)}, bf16[104,640]{1,0:T(8,128)(2,1)S(1)}, u32[]{:S(2)}, u32[]{:S(2)}) collective-permute-start(bf16[104,640]{1,0:T(8,128)(2,1)S(1)} %get-tuple-element.131), channel_id=1, source_target_pairs={{0,6},{2,4},{4,2},{6,0},{1,7},{3,5},{5,3},{7,1},{8,14},{10,12},{12... | collective-permute-start | bytes 399368 | tf_op jit(solution)/shard_map/ppermute | solution.py:24
  162.1 32.3 %collective-permute-start.26 = (bf16[104,640]{1,0:T(8,128)(2,1)S(1)}, bf16[104,640]{1,0:T(8,128)(2,1)S(1)}, u32[]{:S(2)}, u32[]{:S(2)}) collective-permute-start(bf16[104,640]{1,0:T(8,128)(2,1)S(1)} %get-tuple-element.132), channel_id=1, source_target_pairs={{0,4},{2,6},{4,0},{6,2},{1,5},{3,7},{5,1},{7,3},{8,12},{10,14},{12... | collective-permute-start | bytes 399368 | tf_op jit(solution)/shard_map/ppermute | solution.py:24
  165.1 8.5 %copy-start.3 = (bf16[1280,640]{1,0:T(8,128)(2,1)S(1)}, bf16[1280,640]{1,0:T(8,128)(2,1)}, u32[]{:S(2)}) copy-start(bf16[1280,640]{1,0:T(8,128)(2,1)} %get-tuple-element.90.weight_ref) | copy-start | bytes 4915204
  165.1 8.5 %copy-start.6 = (f32[24,640]{1,0:T(8,128)S(1)}, f32[24,640]{1,0:T(8,128)}, u32[]{:S(2)}) copy-start(f32[24,640]{1,0:T(8,128)} %get-tuple-element.91.top_sums_ref) | copy-start | bytes 184324
  165.1 8.5 %copy-start.7 = (f32[8,1280]{1,0:T(8,128)S(1)}, f32[8,1280]{1,0:T(8,128)}, u32[]{:S(2)}) copy-start(f32[8,1280]{1,0:T(8,128)} %get-tuple-element.93.cot_sums_ref) | copy-start | bytes 122884
  165.3 29.2 %collective-permute-start.24 = (bf16[4,2,40,640]{3,2,1,0:T(8,128)(2,1)S(1)}, bf16[4,2,40,640]{3,2,1,0:T(8,128)(2,1)S(1)}, u32[]{:S(2)}, u32[]{:S(2)}) collective-permute-start(bf16[4,2,40,640]{3,2,1,0:T(8,128)(2,1)S(1)} %get-tuple-element.128), channel_id=1, source_target_pairs={{0,24},{8,16},{16,8},{24,0},{1,25},{9,17},{17,9},{25,1},{2,26},{10... | collective-permute-start | bytes 1228808 | tf_op jit(solution)/shard_map/ppermute | solution.py:24
  166.9 27.6 %collective-permute-start.23 = (bf16[4,2,40,640]{3,2,1,0:T(8,128)(2,1)S(1)}, bf16[4,2,40,640]{3,2,1,0:T(8,128)(2,1)S(1)}, u32[]{:S(2)}, u32[]{:S(2)}) collective-permute-start(bf16[4,2,40,640]{3,2,1,0:T(8,128)(2,1)S(1)} %get-tuple-element.129), channel_id=1, source_target_pairs={{0,16},{8,24},{16,0},{24,8},{1,17},{9,25},{17,1},{25,9},{2,18},{10... | collective-permute-start | bytes 1228808 | tf_op jit(solution)/shard_map/ppermute | solution.py:24
  168.3 26.2 %collective-permute-start.22 = (bf16[4,2,40,640]{3,2,1,0:T(8,128)(2,1)S(1)}, bf16[4,2,40,640]{3,2,1,0:T(8,128)(2,1)S(1)}, u32[]{:S(2)}, u32[]{:S(2)}) collective-permute-start(bf16[4,2,40,640]{3,2,1,0:T(8,128)(2,1)S(1)} %get-tuple-element.130), channel_id=1, source_target_pairs={{0,8},{8,0},{16,24},{24,16},{1,9},{9,1},{17,25},{25,17},{2,10},{10... | collective-permute-start | bytes 1228808 | tf_op jit(solution)/shard_map/ppermute | solution.py:24
  168.9 25.6 %collective-permute-start.25 = (bf16[104,640]{1,0:T(8,128)(2,1)S(1)}, bf16[104,640]{1,0:T(8,128)(2,1)S(1)}, u32[]{:S(2)}, u32[]{:S(2)}) collective-permute-start(bf16[104,640]{1,0:T(8,128)(2,1)S(1)} %get-tuple-element.133), channel_id=1, source_target_pairs={{0,2},{2,0},{4,6},{6,4},{1,3},{3,1},{5,7},{7,5},{8,10},{10,8},{12,... | collective-permute-start | bytes 399368 | tf_op jit(solution)/shard_map/ppermute | solution.py:24
  195.5 3.6 %collective-permute-start.31 = (f32[4,4,16,128]{3,2,1,0:T(8,128)S(1)}, f32[4,4,16,128]{3,2,1,0:T(8,128)S(1)}, u32[]{:S(2)}, u32[]{:S(2)}) collective-permute-start(f32[4,4,16,128]{3,2,1,0:T(8,128)S(1)} %get-tuple-element.111), channel_id=1, source_target_pairs={{0,1},{1,0},{2,3},{3,2},{4,5},{5,4},{6,7},{7,6},{8,9},{9,8},{10,11... | collective-permute-start | bytes 393224 | tf_op jit(solution)/shard_map/ppermute | solution.py:24
  195.5 6.6 %collective-permute-start.28 = (bf16[2,40,640]{2,1,0:T(8,128)(2,1)S(1)}, bf16[2,40,640]{2,1,0:T(8,128)(2,1)S(1)}, u32[]{:S(2)}, u32[]{:S(2)}) collective-permute-start(bf16[2,40,640]{2,1,0:T(8,128)(2,1)S(1)} %get-tuple-element.134), channel_id=1, source_target_pairs={{0,2},{2,0},{4,6},{6,4},{1,3},{3,1},{5,7},{7,5},{8,10},{10,8},{12,... | collective-permute-start | bytes 307208 | tf_op jit(solution)/shard_map/ppermute | solution.py:24
  195.7 8.4 %collective-permute-start.30 = (bf16[2,40,640]{2,1,0:T(8,128)(2,1)S(1)}, bf16[2,40,640]{2,1,0:T(8,128)(2,1)S(1)}, u32[]{:S(2)}, u32[]{:S(2)}) collective-permute-start(bf16[2,40,640]{2,1,0:T(8,128)(2,1)S(1)} %get-tuple-element.135), channel_id=1, source_target_pairs={{0,6},{2,4},{4,2},{6,0},{1,7},{3,5},{5,3},{7,1},{8,14},{10,12},{12... | collective-permute-start | bytes 307208 | tf_op jit(solution)/shard_map/ppermute | solution.py:24
  198.1 10.5 %collective-permute-start.29 = (bf16[2,40,640]{2,1,0:T(8,128)(2,1)S(1)}, bf16[2,40,640]{2,1,0:T(8,128)(2,1)S(1)}, u32[]{:S(2)}, u32[]{:S(2)}) collective-permute-start(bf16[2,40,640]{2,1,0:T(8,128)(2,1)S(1)} %get-tuple-element.136), channel_id=1, source_target_pairs={{0,4},{2,6},{4,0},{6,2},{1,5},{3,7},{5,1},{7,3},{8,12},{10,14},{12... | collective-permute-start | bytes 307208 | tf_op jit(solution)/shard_map/ppermute | solution.py:24
  199.1 9.6 %collective-permute-start.33 = (f32[4,16,128]{2,1,0:T(8,128)S(1)}, f32[4,16,128]{2,1,0:T(8,128)S(1)}, u32[]{:S(2)}, u32[]{:S(2)}) collective-permute-start(f32[4,16,128]{2,1,0:T(8,128)S(1)} %get-tuple-element.139), channel_id=1, source_target_pairs={{0,16},{8,24},{16,0},{24,8},{1,17},{9,25},{17,1},{25,9},{2,18},{10... | collective-permute-start | bytes 98312 | tf_op jit(solution)/shard_map/ppermute | solution.py:24
  200.5 8.2 %collective-permute-start.34 = (f32[4,16,128]{2,1,0:T(8,128)S(1)}, f32[4,16,128]{2,1,0:T(8,128)S(1)}, u32[]{:S(2)}, u32[]{:S(2)}) collective-permute-start(f32[4,16,128]{2,1,0:T(8,128)S(1)} %get-tuple-element.140), channel_id=1, source_target_pairs={{0,24},{8,16},{16,8},{24,0},{1,25},{9,17},{17,9},{25,1},{2,26},{10... | collective-permute-start | bytes 98312 | tf_op jit(solution)/shard_map/ppermute | solution.py:24
  202.1 6.6 %collective-permute-start.32 = (f32[4,16,128]{2,1,0:T(8,128)S(1)}, f32[4,16,128]{2,1,0:T(8,128)S(1)}, u32[]{:S(2)}, u32[]{:S(2)}) collective-permute-start(f32[4,16,128]{2,1,0:T(8,128)S(1)} %get-tuple-element.141), channel_id=1, source_target_pairs={{0,8},{8,0},{16,24},{24,16},{1,9},{9,1},{17,25},{25,17},{2,10},{10... | collective-permute-start | bytes 98312 | tf_op jit(solution)/shard_map/ppermute | solution.py:24
  208.8 4.6 %collective-permute-start.36 = (f32[16,128]{1,0:T(8,128)S(1)}, f32[16,128]{1,0:T(8,128)S(1)}, u32[]{:S(2)}, u32[]{:S(2)}) collective-permute-start(f32[16,128]{1,0:T(8,128)S(1)} %get-tuple-element.142), channel_id=1, source_target_pairs={{0,4},{2,6},{4,0},{6,2},{1,5},{3,7},{5,1},{7,3},{8,12},{10,14},{12... | collective-permute-start | bytes 24584 | tf_op jit(solution)/shard_map/ppermute | solution.py:24
  208.9 5.5 %collective-permute-start.37 = (f32[16,128]{1,0:T(8,128)S(1)}, f32[16,128]{1,0:T(8,128)S(1)}, u32[]{:S(2)}, u32[]{:S(2)}) collective-permute-start(f32[16,128]{1,0:T(8,128)S(1)} %get-tuple-element.143), channel_id=1, source_target_pairs={{0,6},{2,4},{4,2},{6,0},{1,7},{3,5},{5,3},{7,1},{8,14},{10,12},{12... | collective-permute-start | bytes 24584 | tf_op jit(solution)/shard_map/ppermute | solution.py:24
  211.4 3.7 %collective-permute-start.35 = (f32[16,128]{1,0:T(8,128)S(1)}, f32[16,128]{1,0:T(8,128)S(1)}, u32[]{:S(2)}, u32[]{:S(2)}) collective-permute-start(f32[16,128]{1,0:T(8,128)S(1)} %get-tuple-element.144), channel_id=1, source_target_pairs={{0,2},{2,0},{4,6},{6,4},{1,3},{3,1},{5,7},{7,5},{8,10},{10,8},{12,... | collective-permute-start | bytes 24584 | tf_op jit(solution)/shard_map/ppermute | solution.py:24
  (4 other events, 4.9 us)

commit v2 on v1

--- a/solution.py
+++ b/solution.py
@@ -122,18 +122,19 @@
     return copies
 
 
-def up_kernel(
-    own_pieces, other_pieces, x_ref, flags_ref, place_ref,
-    act_ref, up_ref, down_ref, wide_ref, narrow_ref, out_ref, mid_ref,
-    hold_ref, up_wide_ref, down_wide_ref, z_ref, next_ref, semaphores,
-):
+def up_kernel(*refs):
+    pieces, rest_refs = refs[: len(refs) - 16], refs[len(refs) - 16 :]
+    (
+        x_ref, flags_ref, place_ref,
+        act_ref, up_ref, down_ref, wide_ref, narrow_ref, out_ref, mid_ref,
+        hold_ref, up_wide_ref, down_wide_ref, z_ref, next_ref, semaphores,
+    ) = rest_refs
     block, width = x_ref.shape
     inner = z_ref.shape[1]
 
     @pl.when(pl.program_id(0) == 0)
     def _():
-        parts = [piece.at[o] for piece in (own_pieces, other_pieces) for o in range(piece.shape[0])]
-        copies = piece_copies(parts, place_ref, hold_ref, semaphores)
+        copies = piece_copies(pieces, place_ref, hold_ref, semaphores)
         for copy in copies:
             copy.start()
         for copy in copies:
@@ -567,7 +568,7 @@
     conv_near += [swap(late_block, name, size, mask) for mask in range(2, size)]
     conv_one = jnp.stack(after(tuple(conv_near), *up_two))
     conv_two = gather_stage(conv_one, axes[0])
-    up_pieces = core_stage([jnp.stack(after(tuple(up_two), *conv_near))], axes)
+    up_pieces = core_stage(up_two[:1] + list(after(tuple(up_two[1:]), *conv_near)), axes)
 
     block, large = 256, 512
     steps = count // block
@@ -576,7 +577,7 @@
     padded = pltpu.VMEM((2, count + 2 * REACH, inner), BF16)
 
     act_one, up_full, down_full, wide, narrow, up_out, mid = call(
-        up_kernel, "up", steps + 1, ("any", "any", "now", "past", "smem"),
+        up_kernel, "up", steps + 1, ("any",) * len(up_pieces) + ("now", "past", "smem"),
         [
             ((count, model), BF16, "now"),
             ((model, inner), BF16, None),

time: 220 us -> 218 us (level)
  starting transfers between devices: 51.8 us -> 46 us
  waiting for transfers between devices: 26.1 us -> 31.9 us
    ppermute x38 -> x41, starting transfers between devices: 51.8 us -> 46 us  [swap(): return lax.ppermute(array, axis, [(k, k ^ mask) for k in range(size)])]
    ppermute x38 -> x41, waiting for transfers between devices: 26.1 us -> 31.9 us  [swap(): return lax.ppermute(array, axis, [(k, k ^ mask) for k in range(size)])]
    another operation x6 -> x5, other arithmetic: 7.04 us -> 5.71 us
    unnamed x60 -> x62, local copies, waits for them, and re-layouts: 5.6 us -> 5.56 us
  transfers between devices with their start and end apart: 38 -> 41, of which waited for: 14 -> 16; matrix products, arithmetic and copies ran while one was open for 4% -> 4% of each run, Pallas kernels for 34% -> 34%
where the time goes in v2:
time: 218 us; the launch traced here: 215 us
  Pallas kernels  116 us (53%)
  starting transfers between devices  46 us (21%)
  waiting for transfers between devices  31.9 us (15%)
  local copies, waits for them, and re-layouts  9.92 us (5%)
  other arithmetic  9.84 us (5%)
    pallas_call x7, Pallas kernels, call(): pl.pallas_call(kernel, name=name, grid=(grid,), in_specs=[spec(a.shape, r...  116 us
    ppermute x41, starting transfers between devices, swap(): return lax.ppermute(array, axis, [(k, k ^ mask) for k in range(size)])  46 us
    ppermute x41, waiting for transfers between devices, swap(): return lax.ppermute(array, axis, [(k, k ^ mask) for k in range(size)])  31.9 us
    another operation x5, other arithmetic  5.71 us
    unnamed x62, local copies, waits for them, and re-layouts  5.56 us
  transfers between devices with their start and end apart: 41, of which 16 were waited for; matrix products, arithmetic and copies ran while one was open for 4% of the time, Pallas kernels for 34%

profile of v2, /device:TPU:0, one launch (start us, length us, event | category | flops | bytes accessed | tf_op | source)
XLA Modules:
  0.0 215.0 jit_solution(12175910040900641910)
XLA Ops:
  0.7 0.9 fusion.22
  1.6 4.1 %collective-permute-start.2 = (bf16[88,640]{1,0:T(8,128)(2,1)S(1)}, bf16[88,640]{1,0:T(8,128)(2,1)S(1)}, u32[]{:S(2)}, u32[]{:S(2)}) collective-permute-start(bf16[88,640]{1,0:T(8,128)(2,1)S(1)} %fusion.22), channel_id=1, source_target_pairs={{0,4},{2,6},{4,0},{6,2},{1,5},{3,7},{5,1},{7,3},{8,12},{10,14},{12... | collective-permute-start | bytes 337928 | tf_op jit(solution)/shard_map/ppermute | solution.py:24
  5.7 1.6 collective-permute-start.1
  7.3 0.9 reshape.253
  8.2 1.0 collective-permute-start
  9.2 0.8 reduce-window.8
  10.2 1.0 fusion.32
  11.2 1.6 collective-permute-done.2
  13.2 2.7 %collective-permute-done.3 = bf16[88,640]{1,0:T(8,128)(2,1)S(1)} collective-permute-done((bf16[88,640]{1,0:T(8,128)(2,1)S(1)}, bf16[88,640]{1,0:T(8,128)(2,1)S(1)}, u32[]{:S(2)}, u32[]{:S(2)}) %collective-permute-start.3) | collective-permute-done | bytes 112672 | tf_op jit(solution)/shard_map/ppermute | solution.py:24
  15.9 2.5 %collective-permute-start.8 = (bf16[4,88,640]{2,1,0:T(8,128)(2,1)S(1)}, bf16[4,88,640]{2,1,0:T(8,128)(2,1)}, u32[]{:S(2)}, u32[]{:S(2)}) collective-permute-start(bf16[4,88,640]{2,1,0:T(8,128)(2,1)S(1)} %pad_maximum_fusion.1.refs_0_), channel_id=1, source_target_pairs={{0,24},{8,16},{16,8},{24,0},{1,25},{9,17},{17,9},{25,1},{2,26},{10... | collective-permute-start | bytes 1351688 | tf_op jit(solution)/shard_map/ppermute | solution.py:24
  18.4 0.5 collective-permute-start.7
  18.9 0.5 collective-permute-start.6
  19.5 2.5 %collective-permute-start.5 = (bf16[104,640]{1,0:T(8,128)(2,1)S(1)}, bf16[104,640]{1,0:T(8,128)(2,1)S(1)}, u32[]{:S(2)}, u32[]{:S(2)}) collective-permute-start(bf16[104,640]{1,0:T(8,128)(2,1)S(1)} %pad.44), channel_id=1, source_target_pairs={{0,6},{2,4},{4,2},{6,0},{1,7},{3,5},{5,3},{7,1},{8,14},{10,12},{12... | collective-permute-start | bytes 399368 | tf_op jit(solution)/shard_map/ppermute | solution.py:24
  22.0 0.5 collective-permute-start.4
  22.6 5.2 %collective-permute-done.5 = bf16[104,640]{1,0:T(8,128)(2,1)S(1)} collective-permute-done((bf16[104,640]{1,0:T(8,128)(2,1)S(1)}, bf16[104,640]{1,0:T(8,128)(2,1)S(1)}, u32[]{:S(2)}, u32[]{:S(2)}) %collective-permute-start.5) | collective-permute-done | bytes 133152 | tf_op jit(solution)/shard_map/ppermute | solution.py:24
  27.8 4.7 %collective-permute-done.4 = bf16[104,640]{1,0:T(8,128)(2,1)S(1)} collective-permute-done((bf16[104,640]{1,0:T(8,128)(2,1)S(1)}, bf16[104,640]{1,0:T(8,128)(2,1)S(1)}, u32[]{:S(2)}, u32[]{:S(2)}) %collective-permute-start.4) | collective-permute-done | bytes 133152 | tf_op jit(solution)/shard_map/ppermute | solution.py:24
  32.5 4.3 %collective-permute-done.7.refs_2_ = bf16[4,88,640]{2,1,0:T(8,128)(2,1)} collective-permute-done((bf16[4,88,640]{2,1,0:T(8,128)(2,1)S(1)}, bf16[4,88,640]{2,1,0:T(8,128)(2,1)}, u32[]{:S(2)}, u32[]{:S(2)}) %collective-permute-start.7) | collective-permute-done | bytes 450592 | tf_op jit(solution)/shard_map/ppermute | solution.py:24
  36.9 0.6 collective-permute-start.14
  37.6 1.8 collective-permute-start.11
  39.4 1.2 collective-permute-start.10
  40.6 0.6 collective-permute-start.9
  42.0 1.1 concatenate.10.refs_9_.refs_12_.flags_ref.now_flags_ref
  43.0 0.6 pad_add_fusion.refs_10_.refs_13_.place_ref
  43.6 18.7 %up.1 = (bf16[2048,1280]{1,0:T(8,128)(2,1)}, bf16[1280,640]{1,0:T(8,128)(2,1)}, bf16[1280,640]{1,0:T(8,128)(2,1)}, f32[8,1280]{1,0:T(8,128)}, f32[8,640]{1,0:T(8...) custom-call(bf16[4,88,640]{2,1,0:T(8,128)(2,1)} %copy-done.14, bf16[4,88,640]{2,1,0:T(8,128)(2,1)} %copy-done.22, ...), custom_call_target="tpu_custom_call" | custom-call | flops 3355443200 | bytes 25358348 | tf_op jit(solution)/shard_map/up/pallas_call | solution.py:484
  62.4 2.0 collective-permute-done.10.refs_2_
  64.5 0.5 collective-permute-start.18
  65.1 1.4 collective-permute-done.17.refs_5_
  66.4 0.8 collective-permute-done.18.refs_6_
  67.2 0.8 collective-permute-done.19.refs_7_
  68.0 0.7 copy-done.21
  68.8 29.0 %conv.1 = (bf16[2048,640]{1,0:T(8,128)(2,1)}, bf16[2048,640]{1,0:T(8,128)(2,1)}, bf16[640,3200]{1,0:T(8,128)(2,1)}, f32[24,640]{1,0:T(8,128)}, f32[8,1280]{1,0:T(8,128)}) custom-call(bf16[4,104,640]{2,1,0:T(8,128)(2,1)} %copy-done.13, bf16[4,104,640]{2,1,0:T(8,128)(2,1)} %copy-done.18, bf16[4,104,640]{2,1,0:T(8,128)(2,1)} %copy-done.17, ...), custom_call_target="tpu_custom_call" | custom-call | flops 11744051200 | bytes 23289868 | tf_op jit(solution)/shard_map/conv/pallas_call | solution.py:484
  97.8 1.9 copy-done.11
  99.7 12.9 %weights.1 = (bf16[4,4,104,640]{3,2,1,0:T(8,128)(2,1)S(1)}, bf16[4,4,104,640]{3,2,1,0:T(8,128)(2,1)S(1)}) custom-call(bf16[2048,640]{1,0:T(8,128)(2,1)S(1)} %copy-done.11, bf16[2048,640]{1,0:T(8,128)(2,1)} %get-tuple-element.71.refs_8_.mid_ref, f32[2048,8]{1,0:T(8,128)S(1)} %copy-done.4, s32[3]{0:T(128)S(1)} %copy-done.8), custom_call_target="tpu_custom_call" | custom-call | flops 8388608000 | bytes 9568268 | tf_op jit(solution)/shard_map/weights/pallas_call | solution.py:484
  112.8 6.0 %output.1 = bf16[2048,1280]{1,0:T(8,128)(2,1)} custom-call(bf16[2048,1280]{1,0:T(8,128)(2,1)S(1)} %bitcast.121, bf16[2048,640]{1,0:T(8,128)(2,1)S(1)} %copy-done, bf16[1280,640]{1,0:T(8,128)(2,1)S(1)} %copy-done.2, f32[8,1280]{1,0:T(8,128)S(1)} %copy-done.5), custom_call_target="tpu_custom_call" | custom-call | flops 3355443200 | bytes 14786560 | tf_op jit(solution)/shard_map/output/pallas_call | solution.py:484
  118.8 2.8 %fusion.26 = (bf16[4,4,104,640]{3,2,1,0:T(8,128)(2,1)S(1)}, f32[4,4,104,640]{3,2,1,0:T(8,128)}) fusion(bf16[4,4,104,640]{3,2,1,0:T(8,128)(2,1)S(1)} %collective-permute-done.20, bf16[4,4,104,640]{3,2,1,0:T(8,128)(2,1)S(1)} %get-tuple-element.85), kind=kLoop, calls=%fused_computation.84 | loop fusion | flops 4259840 | bytes 10649600 | tf_op jit(solution)/shard_map/convert.13
  121.8 1.8 collective-permute-start.23
  123.6 1.2 collective-permute-start.22
  124.8 0.5 collective-permute-start.21
  125.3 2.6 %copy-done.9 = f32[2048,640]{1,0:T(8,128)S(1)} copy-done((f32[2048,640]{1,0:T(8,128)S(1)}, f32[2048,640]{1,0:T(8,128)}, u32[]{:S(2)}) %copy-start.9) | copy-done | bytes 5242904
  128.0 17.6 %mid_grad.1 = (bf16[2048,640]{1,0:T(8,128)(2,1)S(1)}, f32[24,640]{1,0:T(8,128)S(1)}) custom-call(bf16[2048,640]{1,0:T(8,128)(2,1)S(1)} %copy-done.11, bf16[640,3200]{1,0:T(8,128)(2,1)S(1)} %copy-done.10, f32[2048,640]{1,0:T(8,128)S(1)} %copy-done.9, f32[8,640]{1,0:T(8,128)S(1)} %copy-done.12, f32[2048,8]{1,0:T(8,128)S(1)} %copy-done.4, f32[2048,8]{1,0:T(8,128)S(1)} %copy-done.4), custom_call_target="tpu_custom_call" | custom-call | flops 8388608000 | bytes 14794752 | tf_op jit(solution)/shard_map/mid_grad/pallas_call | solution.py:484
  145.7 10.8 %up_weight.1 = (bf16[4,4,2,40,640]{4,3,2,1,0:T(8,128)(2,1)S(1)}, bf16[4,4,2,40,640]{4,3,2,1,0:T(8,128)(2,1)S(1)}) custom-call(bf16[2048,1280]{1,0:T(8,128)(2,1)S(1)} %bitcast.125, bf16[2048,1280]{1,0:T(8,128)(2,1)S(1)} %bitcast.123, bf16[2048,640]{1,0:T(8,128)(2,1)S(1)} %get-tuple-element.87.low_ref.up_low_ref, bf16[2048,640]{1,0:T(8,128)(2,1)S(1)} %copy-done.1, ...), custom_call_target="tpu_custom_call" | custom-call | flops 1 | bytes 1 | tf_op jit(solution)/shard_map/up_weight/pallas_call | solution.py:484
  156.6 1.5 fusion.29
  158.2 2.5 %collective-permute-start.30 = (bf16[104,640]{1,0:T(8,128)(2,1)S(1)}, bf16[104,640]{1,0:T(8,128)(2,1)S(1)}, u32[]{:S(2)}, u32[]{:S(2)}) collective-permute-start(bf16[104,640]{1,0:T(8,128)(2,1)S(1)} %get-tuple-element.129), channel_id=1, source_target_pairs={{0,6},{2,4},{4,2},{6,0},{1,7},{3,5},{5,3},{7,1},{8,14},{10,12},{12... | collective-permute-start | bytes 399368 | tf_op jit(solution)/shard_map/ppermute | solution.py:24
  160.7 2.6 %collective-permute-start.29 = (bf16[104,640]{1,0:T(8,128)(2,1)S(1)}, bf16[104,640]{1,0:T(8,128)(2,1)S(1)}, u32[]{:S(2)}, u32[]{:S(2)}) collective-permute-start(bf16[104,640]{1,0:T(8,128)(2,1)S(1)} %get-tuple-element.130), channel_id=1, source_target_pairs={{0,4},{2,6},{4,0},{6,2},{1,5},{3,7},{5,1},{7,3},{8,12},{10,14},{12... | collective-permute-start | bytes 399368 | tf_op jit(solution)/shard_map/ppermute | solution.py:24
  163.9 1.8 collective-permute-start.27
  165.7 1.2 collective-permute-start.26
  166.9 0.6 collective-permute-start.25
  167.5 4.8 %collective-permute-start.28 = (bf16[104,640]{1,0:T(8,128)(2,1)S(1)}, bf16[104,640]{1,0:T(8,128)(2,1)S(1)}, u32[]{:S(2)}, u32[]{:S(2)}) collective-permute-start(bf16[104,640]{1,0:T(8,128)(2,1)S(1)} %get-tuple-element.131), channel_id=1, source_target_pairs={{0,2},{2,0},{4,6},{6,4},{1,3},{3,1},{5,7},{7,5},{8,10},{10,8},{12,... | collective-permute-start | bytes 399368 | tf_op jit(solution)/shard_map/ppermute | solution.py:24
  172.3 20.7 %input_grad.1 = (f32[2048,1280]{1,0:T(8,128)}, f32[4,4,16,128]{3,2,1,0:T(8,128)S(1)}, f32[4,4,16,128]{3,2,1,0:T(8,128)S(1)}) custom-call(bf16[2048,640]{1,0:T(8,128)(2,1)S(1)} %get-tuple-element.87.low_ref.up_low_ref, bf16[1280,640]{1,0:T(8,128)(2,1)S(1)} %copy-done.3, bf16[2048,1280]{1,0:T(8,128)(2,1)S(1)} %bitcast.121, bf16[2048,1280]{1,0:T(8,128)(2,1)S(1)} %bitcast.123, ...), custom_call_target="tpu_custom_call" | custom-call | flops 3355443200 | bytes 25698316 | tf_op jit(solution)/shard_map/input_grad/pallas_call | solution.py:484
  193.3 0.7 reshape.256
  194.3 2.5 %collective-permute-start.33 = (bf16[2,40,640]{2,1,0:T(8,128)(2,1)S(1)}, bf16[2,40,640]{2,1,0:T(8,128)(2,1)S(1)}, u32[]{:S(2)}, u32[]{:S(2)}) collective-permute-start(bf16[2,40,640]{2,1,0:T(8,128)(2,1)S(1)} %get-tuple-element.133), channel_id=1, source_target_pairs={{0,6},{2,4},{4,2},{6,0},{1,7},{3,5},{5,3},{7,1},{8,14},{10,12},{12... | collective-permute-start | bytes 307208 | tf_op jit(solution)/shard_map/ppermute | solution.py:24
  196.7 0.9 collective-permute-start.32
  197.7 1.6 collective-permute-start.36
  199.3 1.4 collective-permute-start.37
  200.7 0.5 collective-permute-start.35
  201.3 1.5 collective-permute-done.33
  202.7 4.5 %collective-permute-done.32 = bf16[2,40,640]{2,1,0:T(8,128)(2,1)S(1)} collective-permute-done((bf16[2,40,640]{2,1,0:T(8,128)(2,1)S(1)}, bf16[2,40,640]{2,1,0:T(8,128)(2,1)S(1)}, u32[]{:S(2)}, u32[]{:S(2)}) %collective-permute-start.32) | collective-permute-done | bytes 102432 | tf_op jit(solution)/shard_map/ppermute | solution.py:24
  207.5 2.5 %collective-permute-start.40 = (f32[16,128]{1,0:T(8,128)S(1)}, f32[16,128]{1,0:T(8,128)S(1)}, u32[]{:S(2)}, u32[]{:S(2)}) collective-permute-start(f32[16,128]{1,0:T(8,128)S(1)} %get-tuple-element.141), channel_id=1, source_target_pairs={{0,6},{2,4},{4,2},{6,0},{1,7},{3,5},{5,3},{7,1},{8,14},{10,12},{12... | collective-permute-start | bytes 24584 | tf_op jit(solution)/shard_map/ppermute | solution.py:24
  210.0 0.9 collective-permute-start.38
  210.9 0.7 slice_bitcast_fusion.13
  212.0 1.0 collective-permute-done.40
  213.0 0.6 collective-permute-done.38
  213.6 0.5 slice_bitcast_fusion.26
  214.2 0.5 slice_bitcast_fusion.27
  (132 shorter events, 4.0 us)
Async XLA Ops:
  0.6 36.2 %copy-start.15 = (s32[2048]{0:T(1024)S(1)}, s32[2048]{0:T(1024)}, u32[]{:S(2)}) copy-start(s32[2048]{0:T(1024)} %param.18) | copy-start | bytes 24580
  1.6 11.3 %collective-permute-start.2 = (bf16[88,640]{1,0:T(8,128)(2,1)S(1)}, bf16[88,640]{1,0:T(8,128)(2,1)S(1)}, u32[]{:S(2)}, u32[]{:S(2)}) collective-permute-start(bf16[88,640]{1,0:T(8,128)(2,1)S(1)} %fusion.22), channel_id=1, source_target_pairs={{0,4},{2,6},{4,0},{6,2},{1,5},{3,7},{5,1},{7,3},{8,12},{10,14},{12... | collective-permute-start | bytes 337928 | tf_op jit(solution)/shard_map/ppermute | solution.py:24
  5.7 7.5 %collective-permute-start.1 = (bf16[88,640]{1,0:T(8,128)(2,1)S(1)}, bf16[88,640]{1,0:T(8,128)(2,1)S(1)}, u32[]{:S(2)}, u32[]{:S(2)}) collective-permute-start(bf16[88,640]{1,0:T(8,128)(2,1)S(1)} %fusion.22), channel_id=1, source_target_pairs={{0,2},{2,0},{4,6},{6,4},{1,3},{3,1},{5,7},{7,5},{8,10},{10,8},{12,... | collective-permute-start | bytes 337928 | tf_op jit(solution)/shard_map/ppermute | solution.py:24
  7.3 8.6 %collective-permute-start.3 = (bf16[88,640]{1,0:T(8,128)(2,1)S(1)}, bf16[88,640]{1,0:T(8,128)(2,1)S(1)}, u32[]{:S(2)}, u32[]{:S(2)}) collective-permute-start(bf16[88,640]{1,0:T(8,128)(2,1)S(1)} %fusion.22), channel_id=1, source_target_pairs={{0,6},{2,4},{4,2},{6,0},{1,7},{3,5},{5,3},{7,1},{8,14},{10,12},{12... | collective-permute-start | bytes 337928 | tf_op jit(solution)/shard_map/ppermute | solution.py:24
  8.2 13.8 %collective-permute-start = (bf16[104,640]{1,0:T(8,128)(2,1)S(1)}, bf16[104,640]{1,0:T(8,128)(2,1)S(1)}, u32[]{:S(2)}, u32[]{:S(2)}) collective-permute-start(bf16[104,640]{1,0:T(8,128)(2,1)S(1)} %pad.44), channel_id=1, source_target_pairs={{0,2},{2,0},{4,6},{6,4},{1,3},{3,1},{5,7},{7,5},{8,10},{10,8},{12,... | collective-permute-start | bytes 399368 | tf_op jit(solution)/shard_map/ppermute | solution.py:24
  15.9 27.7 %copy-start.14 = (bf16[4,88,640]{2,1,0:T(8,128)(2,1)}, bf16[4,88,640]{2,1,0:T(8,128)(2,1)S(1)}, u32[]{:S(2)}) copy-start(bf16[4,88,640]{2,1,0:T(8,128)(2,1)S(1)} %pad_maximum_fusion.1.refs_0_) | copy-start | bytes 1351684
  15.9 16.5 %collective-permute-start.8 = (bf16[4,88,640]{2,1,0:T(8,128)(2,1)S(1)}, bf16[4,88,640]{2,1,0:T(8,128)(2,1)}, u32[]{:S(2)}, u32[]{:S(2)}) collective-permute-start(bf16[4,88,640]{2,1,0:T(8,128)(2,1)S(1)} %pad_maximum_fusion.1.refs_0_), channel_id=1, source_target_pairs={{0,24},{8,16},{16,8},{24,0},{1,25},{9,17},{17,9},{25,1},{2,26},{10... | collective-permute-start | bytes 1351688 | tf_op jit(solution)/shard_map/ppermute | solution.py:24
  18.4 18.4 %collective-permute-start.7 = (bf16[4,88,640]{2,1,0:T(8,128)(2,1)S(1)}, bf16[4,88,640]{2,1,0:T(8,128)(2,1)}, u32[]{:S(2)}, u32[]{:S(2)}) collective-permute-start(bf16[4,88,640]{2,1,0:T(8,128)(2,1)S(1)} %pad_maximum_fusion.1.refs_0_), channel_id=1, source_target_pairs={{0,16},{8,24},{16,0},{24,8},{1,17},{9,25},{17,1},{25,9},{2,18},{10... | collective-permute-start | bytes 1351688 | tf_op jit(solution)/shard_map/ppermute | solution.py:24
  18.9 17.9 %collective-permute-start.6 = (bf16[4,88,640]{2,1,0:T(8,128)(2,1)S(1)}, bf16[4,88,640]{2,1,0:T(8,128)(2,1)S(1)}, u32[]{:S(2)}, u32[]{:S(2)}) collective-permute-start(bf16[4,88,640]{2,1,0:T(8,128)(2,1)S(1)} %pad_maximum_fusion.1.refs_0_), channel_id=1, source_target_pairs={{0,8},{8,0},{16,24},{24,16},{1,9},{9,1},{17,25},{25,17},{2,10},{10... | collective-permute-start | bytes 1351688 | tf_op jit(solution)/shard_map/ppermute | solution.py:24
  19.5 8.3 %collective-permute-start.5 = (bf16[104,640]{1,0:T(8,128)(2,1)S(1)}, bf16[104,640]{1,0:T(8,128)(2,1)S(1)}, u32[]{:S(2)}, u32[]{:S(2)}) collective-permute-start(bf16[104,640]{1,0:T(8,128)(2,1)S(1)} %pad.44), channel_id=1, source_target_pairs={{0,6},{2,4},{4,2},{6,0},{1,7},{3,5},{5,3},{7,1},{8,14},{10,12},{12... | collective-permute-start | bytes 399368 | tf_op jit(solution)/shard_map/ppermute | solution.py:24
  22.0 10.4 %collective-permute-start.4 = (bf16[104,640]{1,0:T(8,128)(2,1)S(1)}, bf16[104,640]{1,0:T(8,128)(2,1)S(1)}, u32[]{:S(2)}, u32[]{:S(2)}) collective-permute-start(bf16[104,640]{1,0:T(8,128)(2,1)S(1)} %pad.44), channel_id=1, source_target_pairs={{0,4},{2,6},{4,0},{6,2},{1,5},{3,7},{5,1},{7,3},{8,12},{10,14},{12... | collective-permute-start | bytes 399368 | tf_op jit(solution)/shard_map/ppermute | solution.py:24
  27.8 11.6 %collective-permute-start.12 = (bf16[4,88,640]{2,1,0:T(8,128)(2,1)S(1)}, bf16[4,88,640]{2,1,0:T(8,128)(2,1)S(1)}, u32[]{:S(2)}, u32[]{:S(2)}) collective-permute-start(bf16[4,88,640]{2,1,0:T(8,128)(2,1)S(1)} %pad_maximum_fusion.1.refs_0_), channel_id=1, source_target_pairs={{0,1},{1,0},{2,3},{3,2},{4,5},{5,4},{6,7},{7,6},{8,9},{9,8},{10,11... | collective-permute-start | bytes 1351688 | tf_op jit(solution)/shard_map/ppermute | solution.py:24
  36.8 3.8 %copy-start.22 = (bf16[4,88,640]{2,1,0:T(8,128)(2,1)}, bf16[4,88,640]{2,1,0:T(8,128)(2,1)S(1)}, u32[]{:S(2)}) copy-start(bf16[4,88,640]{2,1,0:T(8,128)(2,1)S(1)} %collective-permute-done.6.refs_1_) | copy-start | bytes 1351684
  36.8 3.8 %collective-permute-start.13 = (bf16[4,88,640]{2,1,0:T(8,128)(2,1)S(1)}, bf16[4,88,640]{2,1,0:T(8,128)(2,1)S(1)}, u32[]{:S(2)}, u32[]{:S(2)}) collective-permute-start(bf16[4,88,640]{2,1,0:T(8,128)(2,1)S(1)} %collective-permute-done.6.refs_1_), channel_id=1, source_target_pairs={{0,1},{1,0},{2,3},{3,2},{4,5},{5,4},{6,7},{7,6},{8,9},{9,8},{10,11... | collective-permute-start | bytes 1351688 | tf_op jit(solution)/shard_map/ppermute | solution.py:24
  36.9 6.8 %collective-permute-start.14 = (bf16[4,88,640]{2,1,0:T(8,128)(2,1)}, bf16[4,88,640]{2,1,0:T(8,128)(2,1)}, u32[]{:S(2)}, u32[]{:S(2)}) collective-permute-start(bf16[4,88,640]{2,1,0:T(8,128)(2,1)} %collective-permute-done.7.refs_2_), channel_id=1, source_target_pairs={{0,1},{1,0},{2,3},{3,2},{4,5},{5,4},{6,7},{7,6},{8,9},{9,8},{10,11... | collective-permute-start | bytes 1351688 | tf_op jit(solution)/shard_map/ppermute | solution.py:24
  37.4 6.2 %collective-permute-start.15 = (bf16[4,88,640]{2,1,0:T(8,128)(2,1)}, bf16[4,88,640]{2,1,0:T(8,128)(2,1)}, u32[]{:S(2)}, u32[]{:S(2)}) collective-permute-start(bf16[4,88,640]{2,1,0:T(8,128)(2,1)} %collective-permute-done.8.refs_3_), channel_id=1, source_target_pairs={{0,1},{1,0},{2,3},{3,2},{4,5},{5,4},{6,7},{7,6},{8,9},{9,8},{10,11... | collective-permute-start | bytes 1351688 | tf_op jit(solution)/shard_map/ppermute | solution.py:24
  37.6 24.8 %copy-start.13 = (bf16[4,104,640]{2,1,0:T(8,128)(2,1)}, bf16[4,104,640]{2,1,0:T(8,128)(2,1)S(1)}, u32[]{:S(2)}) copy-start(bf16[4,104,640]{2,1,0:T(8,128)(2,1)S(1)} %pad_maximum_fusion.refs_0_) | copy-start | bytes 1597444
  37.6 24.8 %collective-permute-start.11 = (bf16[4,104,640]{2,1,0:T(8,128)(2,1)S(1)}, bf16[4,104,640]{2,1,0:T(8,128)(2,1)S(1)}, u32[]{:S(2)}, u32[]{:S(2)}) collective-permute-start(bf16[4,104,640]{2,1,0:T(8,128)(2,1)S(1)} %pad_maximum_fusion.refs_0_), channel_id=1, source_target_pairs={{0,24},{8,16},{16,8},{24,0},{1,25},{9,17},{17,9},{25,1},{2,26},{10... | collective-permute-start | bytes 1597448 | tf_op jit(solution)/shard_map/ppermute | solution.py:24
  39.4 25.0 %collective-permute-start.10 = (bf16[4,104,640]{2,1,0:T(8,128)(2,1)S(1)}, bf16[4,104,640]{2,1,0:T(8,128)(2,1)S(1)}, u32[]{:S(2)}, u32[]{:S(2)}) collective-permute-start(bf16[4,104,640]{2,1,0:T(8,128)(2,1)S(1)} %pad_maximum_fusion.refs_0_), channel_id=1, source_target_pairs={{0,16},{8,24},{16,0},{24,8},{1,17},{9,25},{17,1},{25,9},{2,18},{10... | collective-permute-start | bytes 1597448 | tf_op jit(solution)/shard_map/ppermute | solution.py:24
  40.6 23.9 %collective-permute-start.9 = (bf16[4,104,640]{2,1,0:T(8,128)(2,1)S(1)}, bf16[4,104,640]{2,1,0:T(8,128)(2,1)S(1)}, u32[]{:S(2)}, u32[]{:S(2)}) collective-permute-start(bf16[4,104,640]{2,1,0:T(8,128)(2,1)S(1)} %pad_maximum_fusion.refs_0_), channel_id=1, source_target_pairs={{0,8},{8,0},{16,24},{24,16},{1,9},{9,1},{17,25},{25,17},{2,10},{10... | collective-permute-start | bytes 1597448 | tf_op jit(solution)/shard_map/ppermute | solution.py:24
  43.6 21.5 %collective-permute-start.16 = (bf16[4,104,640]{2,1,0:T(8,128)(2,1)S(1)}, bf16[4,104,640]{2,1,0:T(8,128)(2,1)}, u32[]{:S(2)}, u32[]{:S(2)}) collective-permute-start(bf16[4,104,640]{2,1,0:T(8,128)(2,1)S(1)} %pad_maximum_fusion.refs_0_), channel_id=1, source_target_pairs={{0,1},{1,0},{2,3},{3,2},{4,5},{5,4},{6,7},{7,6},{8,9},{9,8},{10,11... | collective-permute-start | bytes 1597448 | tf_op jit(solution)/shard_map/ppermute | solution.py:24
  62.4 6.4 %copy-start.16 = (bf16[4,104,640]{2,1,0:T(8,128)(2,1)}, bf16[4,104,640]{2,1,0:T(8,128)(2,1)S(1)}, u32[]{:S(2)}) copy-start(bf16[4,104,640]{2,1,0:T(8,128)(2,1)S(1)} %collective-permute-done.11.refs_3_) | copy-start | bytes 1597444
  64.4 4.4 %copy-start.17 = (bf16[4,104,640]{2,1,0:T(8,128)(2,1)}, bf16[4,104,640]{2,1,0:T(8,128)(2,1)S(1)}, u32[]{:S(2)}) copy-start(bf16[4,104,640]{2,1,0:T(8,128)(2,1)S(1)} %collective-permute-done.10.refs_2_) | copy-start | bytes 1597444
  64.5 1.9 collective-permute-start.17
  64.5 2.7 %collective-permute-start.18 = (bf16[4,104,640]{2,1,0:T(8,128)(2,1)S(1)}, bf16[4,104,640]{2,1,0:T(8,128)(2,1)S(1)}, u32[]{:S(2)}, u32[]{:S(2)}) collective-permute-start(bf16[4,104,640]{2,1,0:T(8,128)(2,1)S(1)} %collective-permute-done.10.refs_2_), channel_id=1, source_target_pairs={{0,1},{1,0},{2,3},{3,2},{4,5},{5,4},{6,7},{7,6},{8,9},{9,8},{10,11... | collective-permute-start | bytes 1597448 | tf_op jit(solution)/shard_map/ppermute | solution.py:24
  65.0 2.9 %collective-permute-start.19 = (bf16[4,104,640]{2,1,0:T(8,128)(2,1)S(1)}, bf16[4,104,640]{2,1,0:T(8,128)(2,1)S(1)}, u32[]{:S(2)}, u32[]{:S(2)}) collective-permute-start(bf16[4,104,640]{2,1,0:T(8,128)(2,1)S(1)} %collective-permute-done.11.refs_3_), channel_id=1, source_target_pairs={{0,1},{1,0},{2,3},{3,2},{4,5},{5,4},{6,7},{7,6},{8,9},{9,8},{10,11... | collective-permute-start | bytes 1597448 | tf_op jit(solution)/shard_map/ppermute | solution.py:24
  68.8 29.0 %copy-start.4 = (f32[2048,8]{1,0:T(8,128)S(1)}, f32[2048,8]{1,0:T(8,128)}, u32[]{:S(2)}) copy-start(f32[2048,8]{1,0:T(8,128)} %concatenate.10.refs_9_.refs_12_.flags_ref.now_flags_ref) | copy-start | bytes 196612
  68.8 29.0 %copy-start.8 = (s32[3]{0:T(128)S(1)}, s32[3]{0:T(128)}, u32[]{:S(2)}) copy-start(s32[3]{0:T(128)} %pad_add_fusion.refs_10_.refs_13_.place_ref) | copy-start | bytes 40
  97.8 15.1 %slice-start = ((s8[5242880]{0:T(1024)(128)(4,1)}), s8[4194304]{0:T(1024)(128)(4,1)S(1)}, s32[]{:S(2)}) async-start(s8[5242880]{0:T(1024)(128)(4,1)} %bitcast.120), calls=%async_computation | async-start | bytes 8388608
  99.7 13.1 %slice-start.1 = ((s8[5242880]{0:T(1024)(128)(4,1)}), s8[1048576]{0:T(1024)(128)(4,1)S(1)}, s32[]{:S(2)}) async-start(s8[5242880]{0:T(1024)(128)(4,1)} %bitcast.120), calls=%async_computation.1 | async-start | bytes 2097152
  99.7 13.1 %copy-start = (bf16[2048,640]{1,0:T(8,128)(2,1)S(1)}, bf16[2048,640]{1,0:T(8,128)(2,1)}, u32[]{:S(2)}) copy-start(bf16[2048,640]{1,0:T(8,128)(2,1)} %get-tuple-element.77.top_ref) | copy-start | bytes 7864324
  99.7 13.1 %copy-start.2 = (bf16[1280,640]{1,0:T(8,128)(2,1)S(1)}, bf16[1280,640]{1,0:T(8,128)(2,1)}, u32[]{:S(2)}) copy-start(bf16[1280,640]{1,0:T(8,128)(2,1)} %get-tuple-element.75.refs_9_.weight_ref) | copy-start | bytes 4915204
  99.7 13.1 %copy-start.5 = (f32[8,1280]{1,0:T(8,128)S(1)}, f32[8,1280]{1,0:T(8,128)}, u32[]{:S(2)}) copy-start(f32[8,1280]{1,0:T(8,128)} %get-tuple-element.81.wide_ref) | copy-start | bytes 122884
  112.6 6.2 %collective-permute-start.20 = (bf16[4,4,104,640]{3,2,1,0:T(8,128)(2,1)S(1)}, bf16[4,4,104,640]{3,2,1,0:T(8,128)(2,1)S(1)}, u32[]{:S(2)}, u32[]{:S(2)}) collective-permute-start(bf16[4,4,104,640]{3,2,1,0:T(8,128)(2,1)S(1)} %get-tuple-element.80), channel_id=1, source_target_pairs={{0,1},{1,0},{2,3},{3,2},{4,5},{5,4},{6,7},{7,6},{8,9},{9,8},{10,11... | collective-permute-start | bytes 6389768 | tf_op jit(solution)/shard_map/ppermute | solution.py:24
  118.8 6.5 %copy-start.10 = (bf16[640,3200]{1,0:T(8,128)(2,1)S(1)}, bf16[640,3200]{1,0:T(8,128)(2,1)}, u32[]{:S(2)}) copy-start(bf16[640,3200]{1,0:T(8,128)(2,1)} %get-tuple-element.82.flat_ref) | copy-start | bytes 12288004
  121.6 3.7 %copy-start.12 = (f32[8,640]{1,0:T(8,128)S(1)}, f32[8,640]{1,0:T(8,128)}, u32[]{:S(2)}) copy-start(f32[8,640]{1,0:T(8,128)} %get-tuple-element.86.refs_11_.narrow_ref) | copy-start | bytes 61444
  121.8 34.7 %collective-permute-start.23 = (bf16[4,104,640]{2,1,0:T(8,128)(2,1)S(1)}, bf16[4,104,640]{2,1,0:T(8,128)(2,1)S(1)}, u32[]{:S(2)}, u32[]{:S(2)}) collective-permute-start(bf16[4,104,640]{2,1,0:T(8,128)(2,1)S(1)} %get-tuple-element.123), channel_id=1, source_target_pairs={{0,24},{8,16},{16,8},{24,0},{1,25},{9,17},{17,9},{25,1},{2,26},{10... | collective-permute-start | bytes 1597448 | tf_op jit(solution)/shard_map/ppermute | solution.py:24
  123.6 32.9 %collective-permute-start.22 = (bf16[4,104,640]{2,1,0:T(8,128)(2,1)S(1)}, bf16[4,104,640]{2,1,0:T(8,128)(2,1)S(1)}, u32[]{:S(2)}, u32[]{:S(2)}) collective-permute-start(bf16[4,104,640]{2,1,0:T(8,128)(2,1)S(1)} %get-tuple-element.124), channel_id=1, source_target_pairs={{0,16},{8,24},{16,0},{24,8},{1,17},{9,25},{17,1},{25,9},{2,18},{10... | collective-permute-start | bytes 1597448 | tf_op jit(solution)/shard_map/ppermute | solution.py:24
  124.8 31.7 %collective-permute-start.21 = (bf16[4,104,640]{2,1,0:T(8,128)(2,1)S(1)}, bf16[4,104,640]{2,1,0:T(8,128)(2,1)S(1)}, u32[]{:S(2)}, u32[]{:S(2)}) collective-permute-start(bf16[4,104,640]{2,1,0:T(8,128)(2,1)S(1)} %get-tuple-element.125), channel_id=1, source_target_pairs={{0,8},{8,0},{16,24},{24,16},{1,9},{9,1},{17,25},{25,17},{2,10},{10... | collective-permute-start | bytes 1597448 | tf_op jit(solution)/shard_map/ppermute | solution.py:24
  125.3 20.3 %slice-start.2 = ((s8[5242880]{0:T(1024)(128)(4,1)}), s8[4194304]{0:T(1024)(128)(4,1)S(1)}, s32[]{:S(2)}) async-start(s8[5242880]{0:T(1024)(128)(4,1)} %bitcast.122), calls=%async_computation.2 | async-start | bytes 8388608
  125.3 20.3 %slice-start.4 = ((s8[5242880]{0:T(1024)(128)(4,1)}), s8[4194304]{0:T(1024)(128)(4,1)S(1)}, s32[]{:S(2)}) async-start(s8[5242880]{0:T(1024)(128)(4,1)} %bitcast.124), calls=%async_computation.4 | async-start | bytes 8388608
  128.0 17.7 %slice-start.3 = ((s8[5242880]{0:T(1024)(128)(4,1)}), s8[1048576]{0:T(1024)(128)(4,1)S(1)}, s32[]{:S(2)}) async-start(s8[5242880]{0:T(1024)(128)(4,1)} %bitcast.122), calls=%async_computation.3 | async-start | bytes 2097152
  128.0 17.7 %copy-start.1 = (bf16[2048,640]{1,0:T(8,128)(2,1)S(1)}, bf16[2048,640]{1,0:T(8,128)(2,1)}, u32[]{:S(2)}) copy-start(bf16[2048,640]{1,0:T(8,128)(2,1)} %get-tuple-element.77.top_ref) | copy-start | bytes 7864324
  128.0 17.7 %slice-start.5 = ((s8[5242880]{0:T(1024)(128)(4,1)}), s8[1048576]{0:T(1024)(128)(4,1)S(1)}, s32[]{:S(2)}) async-start(s8[5242880]{0:T(1024)(128)(4,1)} %bitcast.124), calls=%async_computation.5 | async-start | bytes 2097152
  156.5 6.8 %collective-permute-start.24 = (bf16[4,4,2,40,640]{4,3,2,1,0:T(8,128)(2,1)S(1)}, bf16[4,4,2,40,640]{4,3,2,1,0:T(8,128)(2,1)S(1)}, u32[]{:S(2)}, u32[]{:S(2)}) collective-permute-start(bf16[4,4,2,40,640]{4,3,2,1,0:T(8,128)(2,1)S(1)} %get-tuple-element.98), channel_id=1, source_target_pairs={{0,1},{1,0},{2,3},{3,2},{4,5},{5,4},{6,7},{7,6},{8,9},{9,8},{10,11... | collective-permute-start | bytes 4915208 | tf_op jit(solution)/shard_map/ppermute | solution.py:24
  158.2 9.3 %collective-permute-start.30 = (bf16[104,640]{1,0:T(8,128)(2,1)S(1)}, bf16[104,640]{1,0:T(8,128)(2,1)S(1)}, u32[]{:S(2)}, u32[]{:S(2)}) collective-permute-start(bf16[104,640]{1,0:T(8,128)(2,1)S(1)} %get-tuple-element.129), channel_id=1, source_target_pairs={{0,6},{2,4},{4,2},{6,0},{1,7},{3,5},{5,3},{7,1},{8,14},{10,12},{12... | collective-permute-start | bytes 399368 | tf_op jit(solution)/shard_map/ppermute | solution.py:24
  160.7 32.3 %collective-permute-start.29 = (bf16[104,640]{1,0:T(8,128)(2,1)S(1)}, bf16[104,640]{1,0:T(8,128)(2,1)S(1)}, u32[]{:S(2)}, u32[]{:S(2)}) collective-permute-start(bf16[104,640]{1,0:T(8,128)(2,1)S(1)} %get-tuple-element.130), channel_id=1, source_target_pairs={{0,4},{2,6},{4,0},{6,2},{1,5},{3,7},{5,1},{7,3},{8,12},{10,14},{12... | collective-permute-start | bytes 399368 | tf_op jit(solution)/shard_map/ppermute | solution.py:24
  163.8 8.5 %copy-start.3 = (bf16[1280,640]{1,0:T(8,128)(2,1)S(1)}, bf16[1280,640]{1,0:T(8,128)(2,1)}, u32[]{:S(2)}) copy-start(bf16[1280,640]{1,0:T(8,128)(2,1)} %get-tuple-element.88.weight_ref) | copy-start | bytes 4915204
  163.8 8.5 %copy-start.6 = (f32[24,640]{1,0:T(8,128)S(1)}, f32[24,640]{1,0:T(8,128)}, u32[]{:S(2)}) copy-start(f32[24,640]{1,0:T(8,128)} %get-tuple-element.89.top_sums_ref) | copy-start | bytes 184324
  163.8 8.5 %copy-start.7 = (f32[8,1280]{1,0:T(8,128)S(1)}, f32[8,1280]{1,0:T(8,128)}, u32[]{:S(2)}) copy-start(f32[8,1280]{1,0:T(8,128)} %get-tuple-element.91.cot_sums_ref) | copy-start | bytes 122884
  163.9 29.1 %collective-permute-start.27 = (bf16[4,2,40,640]{3,2,1,0:T(8,128)(2,1)S(1)}, bf16[4,2,40,640]{3,2,1,0:T(8,128)(2,1)S(1)}, u32[]{:S(2)}, u32[]{:S(2)}) collective-permute-start(bf16[4,2,40,640]{3,2,1,0:T(8,128)(2,1)S(1)} %get-tuple-element.126), channel_id=1, source_target_pairs={{0,24},{8,16},{16,8},{24,0},{1,25},{9,17},{17,9},{25,1},{2,26},{10... | collective-permute-start | bytes 1228808 | tf_op jit(solution)/shard_map/ppermute | solution.py:24
  165.7 27.4 %collective-permute-start.26 = (bf16[4,2,40,640]{3,2,1,0:T(8,128)(2,1)S(1)}, bf16[4,2,40,640]{3,2,1,0:T(8,128)(2,1)S(1)}, u32[]{:S(2)}, u32[]{:S(2)}) collective-permute-start(bf16[4,2,40,640]{3,2,1,0:T(8,128)(2,1)S(1)} %get-tuple-element.127), channel_id=1, source_target_pairs={{0,16},{8,24},{16,0},{24,8},{1,17},{9,25},{17,1},{25,9},{2,18},{10... | collective-permute-start | bytes 1228808 | tf_op jit(solution)/shard_map/ppermute | solution.py:24
  166.9 26.2 %collective-permute-start.25 = (bf16[4,2,40,640]{3,2,1,0:T(8,128)(2,1)S(1)}, bf16[4,2,40,640]{3,2,1,0:T(8,128)(2,1)S(1)}, u32[]{:S(2)}, u32[]{:S(2)}) collective-permute-start(bf16[4,2,40,640]{3,2,1,0:T(8,128)(2,1)S(1)} %get-tuple-element.128), channel_id=1, source_target_pairs={{0,8},{8,0},{16,24},{24,16},{1,9},{9,1},{17,25},{25,17},{2,10},{10... | collective-permute-start | bytes 1228808 | tf_op jit(solution)/shard_map/ppermute | solution.py:24
  167.5 25.5 %collective-permute-start.28 = (bf16[104,640]{1,0:T(8,128)(2,1)S(1)}, bf16[104,640]{1,0:T(8,128)(2,1)S(1)}, u32[]{:S(2)}, u32[]{:S(2)}) collective-permute-start(bf16[104,640]{1,0:T(8,128)(2,1)S(1)} %get-tuple-element.131), channel_id=1, source_target_pairs={{0,2},{2,0},{4,6},{6,4},{1,3},{3,1},{5,7},{7,5},{8,10},{10,8},{12,... | collective-permute-start | bytes 399368 | tf_op jit(solution)/shard_map/ppermute | solution.py:24
  194.1 3.6 %collective-permute-start.34 = (f32[4,4,16,128]{3,2,1,0:T(8,128)S(1)}, f32[4,4,16,128]{3,2,1,0:T(8,128)S(1)}, u32[]{:S(2)}, u32[]{:S(2)}) collective-permute-start(f32[4,4,16,128]{3,2,1,0:T(8,128)S(1)} %get-tuple-element.109), channel_id=1, source_target_pairs={{0,1},{1,0},{2,3},{3,2},{4,5},{5,4},{6,7},{7,6},{8,9},{9,8},{10,11... | collective-permute-start | bytes 393224 | tf_op jit(solution)/shard_map/ppermute | solution.py:24
  194.1 6.6 %collective-permute-start.31 = (bf16[2,40,640]{2,1,0:T(8,128)(2,1)S(1)}, bf16[2,40,640]{2,1,0:T(8,128)(2,1)S(1)}, u32[]{:S(2)}, u32[]{:S(2)}) collective-permute-start(bf16[2,40,640]{2,1,0:T(8,128)(2,1)S(1)} %get-tuple-element.132), channel_id=1, source_target_pairs={{0,2},{2,0},{4,6},{6,4},{1,3},{3,1},{5,7},{7,5},{8,10},{10,8},{12,... | collective-permute-start | bytes 307208 | tf_op jit(solution)/shard_map/ppermute | solution.py:24
  194.3 8.4 %collective-permute-start.33 = (bf16[2,40,640]{2,1,0:T(8,128)(2,1)S(1)}, bf16[2,40,640]{2,1,0:T(8,128)(2,1)S(1)}, u32[]{:S(2)}, u32[]{:S(2)}) collective-permute-start(bf16[2,40,640]{2,1,0:T(8,128)(2,1)S(1)} %get-tuple-element.133), channel_id=1, source_target_pairs={{0,6},{2,4},{4,2},{6,0},{1,7},{3,5},{5,3},{7,1},{8,14},{10,12},{12... | collective-permute-start | bytes 307208 | tf_op jit(solution)/shard_map/ppermute | solution.py:24
  196.7 10.5 %collective-permute-start.32 = (bf16[2,40,640]{2,1,0:T(8,128)(2,1)S(1)}, bf16[2,40,640]{2,1,0:T(8,128)(2,1)S(1)}, u32[]{:S(2)}, u32[]{:S(2)}) collective-permute-start(bf16[2,40,640]{2,1,0:T(8,128)(2,1)S(1)} %get-tuple-element.134), channel_id=1, source_target_pairs={{0,4},{2,6},{4,0},{6,2},{1,5},{3,7},{5,1},{7,3},{8,12},{10,14},{12... | collective-permute-start | bytes 307208 | tf_op jit(solution)/shard_map/ppermute | solution.py:24
  197.7 9.6 %collective-permute-start.36 = (f32[4,16,128]{2,1,0:T(8,128)S(1)}, f32[4,16,128]{2,1,0:T(8,128)S(1)}, u32[]{:S(2)}, u32[]{:S(2)}) collective-permute-start(f32[4,16,128]{2,1,0:T(8,128)S(1)} %get-tuple-element.137), channel_id=1, source_target_pairs={{0,16},{8,24},{16,0},{24,8},{1,17},{9,25},{17,1},{25,9},{2,18},{10... | collective-permute-start | bytes 98312 | tf_op jit(solution)/shard_map/ppermute | solution.py:24
  199.3 8.0 %collective-permute-start.37 = (f32[4,16,128]{2,1,0:T(8,128)S(1)}, f32[4,16,128]{2,1,0:T(8,128)S(1)}, u32[]{:S(2)}, u32[]{:S(2)}) collective-permute-start(f32[4,16,128]{2,1,0:T(8,128)S(1)} %get-tuple-element.138), channel_id=1, source_target_pairs={{0,24},{8,16},{16,8},{24,0},{1,25},{9,17},{17,9},{25,1},{2,26},{10... | collective-permute-start | bytes 98312 | tf_op jit(solution)/shard_map/ppermute | solution.py:24
  200.7 6.6 %collective-permute-start.35 = (f32[4,16,128]{2,1,0:T(8,128)S(1)}, f32[4,16,128]{2,1,0:T(8,128)S(1)}, u32[]{:S(2)}, u32[]{:S(2)}) collective-permute-start(f32[4,16,128]{2,1,0:T(8,128)S(1)} %get-tuple-element.139), channel_id=1, source_target_pairs={{0,8},{8,0},{16,24},{24,16},{1,9},{9,1},{17,25},{25,17},{2,10},{10... | collective-permute-start | bytes 98312 | tf_op jit(solution)/shard_map/ppermute | solution.py:24
  207.3 4.6 %collective-permute-start.39 = (f32[16,128]{1,0:T(8,128)S(1)}, f32[16,128]{1,0:T(8,128)S(1)}, u32[]{:S(2)}, u32[]{:S(2)}) collective-permute-start(f32[16,128]{1,0:T(8,128)S(1)} %get-tuple-element.140), channel_id=1, source_target_pairs={{0,4},{2,6},{4,0},{6,2},{1,5},{3,7},{5,1},{7,3},{8,12},{10,14},{12... | collective-permute-start | bytes 24584 | tf_op jit(solution)/shard_map/ppermute | solution.py:24
  207.5 5.5 %collective-permute-start.40 = (f32[16,128]{1,0:T(8,128)S(1)}, f32[16,128]{1,0:T(8,128)S(1)}, u32[]{:S(2)}, u32[]{:S(2)}) collective-permute-start(f32[16,128]{1,0:T(8,128)S(1)} %get-tuple-element.141), channel_id=1, source_target_pairs={{0,6},{2,4},{4,2},{6,0},{1,7},{3,5},{5,3},{7,1},{8,14},{10,12},{12... | collective-permute-start | bytes 24584 | tf_op jit(solution)/shard_map/ppermute | solution.py:24
  210.0 3.7 %collective-permute-start.38 = (f32[16,128]{1,0:T(8,128)S(1)}, f32[16,128]{1,0:T(8,128)S(1)}, u32[]{:S(2)}, u32[]{:S(2)}) collective-permute-start(f32[16,128]{1,0:T(8,128)S(1)} %get-tuple-element.142), channel_id=1, source_target_pairs={{0,2},{2,0},{4,6},{6,4},{1,3},{3,1},{5,7},{7,5},{8,10},{10,8},{12,... | collective-permute-start | bytes 24584 | tf_op jit(solution)/shard_map/ppermute | solution.py:24
  (8 other events, 13.7 us)
